TPU v7x, 32 devices: a whole 2x2x4 slice. The times are simulated.
32 devices in a mesh: batch: 8 (over y, x, core), chan: 4 (over z).
Axes of the slice: x: 2, y: 2, z: 4, core: 2. Of those that a mesh axis runs over, the one named last changes fastest.
Arguments:
- image_big: bfloat16 [512, 14, 14, 256], P(('batch', 'chan')), may hold values from -40 to 40
- image_small: bfloat16 [1024, 6, 6, 256], P(('batch', 'chan')), may hold values from -40 to 40
- slope_big: bfloat16 [512, 7, 7, 512], P('batch', None, None, 'chan'), may hold values from -40 to 40
- slope_small: bfloat16 [1024, 3, 3, 512], P('batch', None, None, 'chan'), may hold values from -40 to 40
- conv1_weight: float32 [3, 3, 256, 512], P(None, None, 'batch', 'chan'), may hold values from -0.125 to 0.125
- conv2_weight: float32 [3, 3, 512, 512], P(None, None, 'batch', 'chan'), may hold values from -0.09375 to 0.09375
- proj_weight: float32 [256, 512], P('batch', 'chan'), may hold values from -0.375 to 0.375
- norm_params: float32 [6, 512], P(None, 'chan'), may hold values from 0.1 to 1.9
- first_conv1: float32 [3, 3, 256, 512], P(None, None, 'batch', 'chan')
- first_conv2: float32 [3, 3, 512, 512], P(None, None, 'batch', 'chan')
- first_proj: float32 [256, 512], P('batch', 'chan')
- first_norms: float32 [6, 512], P(None, 'chan')
- second_conv1: float32 [3, 3, 256, 512], P(None, None, 'batch', 'chan'), as said below
- second_conv2: float32 [3, 3, 512, 512], P(None, None, 'batch', 'chan'), as said below
- second_proj: float32 [256, 512], P('batch', 'chan'), as said below
- second_norms: float32 [6, 512], P(None, 'chan'), as said below
Outputs:
- out_big: bfloat16 [512, 7, 7, 512], P('batch', None, None, 'chan')
- out_small: bfloat16 [1024, 3, 3, 512], P('batch', None, None, 'chan')
- grad_big: bfloat16 [512, 14, 14, 256], P(('batch', 'chan'))
- grad_small: bfloat16 [1024, 6, 6, 256], P(('batch', 'chan'))
- grad_conv1: float32 [3, 3, 256, 512], P(None, None, 'batch', 'chan')
- grad_conv2: float32 [3, 3, 512, 512], P(None, None, 'batch', 'chan')
- grad_proj: float32 [256, 512], P('batch', 'chan')
- grad_norms: float32 [6, 512], P(None, 'chan')
- new_conv1: float32 [3, 3, 256, 512], P(None, None, 'batch', 'chan')
- new_conv2: float32 [3, 3, 512, 512], P(None, None, 'batch', 'chan')
- new_proj: float32 [256, 512], P('batch', 'chan')
- new_norms: float32 [6, 512], P(None, 'chan')
- moment_conv1: float32 [3, 3, 256, 512], P(None, None, 'batch', 'chan')
- moment_conv2: float32 [3, 3, 512, 512], P(None, None, 'batch', 'chan')
- moment_proj: float32 [256, 512], P('batch', 'chan')
- moment_norms: float32 [6, 512], P(None, 'chan')
- square_conv1: float32 [3, 3, 256, 512], P(None, None, 'batch', 'chan')
- square_conv2: float32 [3, 3, 512, 512], P(None, None, 'batch', 'chan')
- square_proj: float32 [256, 512], P('batch', 'chan')
- square_norms: float32 [6, 512], P(None, 'chan')
Inputs may be any that keep to these rules, and one draw needn't show every extreme that they name: `second_conv1`: Positive. `second_conv2`: Positive. `second_proj`: Positive. `second_norms`: Positive.
All inputs are finite; a program needn't handle non-finite values.
Results may differ from a plain program's by a relative error of at most 0.0078.
Values may be sent and summed in bfloat16 or wider, within the bound.
A program may use at most 320 MiB of HBM per device.

v0:
```python
import jax
import jax.numpy as jnp
from jax import lax
from jax.sharding import PartitionSpec as P

C_IN = 256
C_OUT = 512
STEP = 5


NORM_EPS = 1e-05
BETA_ONE = 0.5
BETA_TWO = 0.5
ADAM_EPS = 1e-08
DECAY = 0.01
NORM_RATE = 0.3


def tap_window(padded, tap_row, tap_col, stride, size_out):
    reach = stride * (size_out - 1) + 1
    return lax.slice(
        padded,
        (0, tap_row, tap_col, 0),
        (padded.shape[0], tap_row + reach, tap_col + reach, padded.shape[3]),
        (1, stride, stride, 1),
    )


def conv_taps(inputs, kernel, stride):
    size_out = (inputs.shape[1] - 1) // stride + 1
    padded = jnp.pad(inputs, ((0, 0), (1, 1), (1, 1), (0, 0)))
    summed = jnp.zeros((inputs.shape[0], size_out, size_out, kernel.shape[3]), jnp.float32)
    for tap_row in range(3):
        for tap_col in range(3):
            window = tap_window(padded, tap_row, tap_col, stride, size_out)
            summed = summed + jnp.einsum(
                "nhwc,co->nhwo",
                window,
                kernel[tap_row, tap_col],
                preferred_element_type=jnp.float32,
            )
    return summed


def kernel_grad(inputs, slope, stride):
    size_out = slope.shape[1]
    padded = jnp.pad(inputs, ((0, 0), (1, 1), (1, 1), (0, 0)))
    tap_rows = []
    for tap_row in range(3):
        across = []
        for tap_col in range(3):
            window = tap_window(padded, tap_row, tap_col, stride, size_out)
            across.append(
                jnp.einsum("nhwc,nhwo->co", window, slope, preferred_element_type=jnp.float32)
            )
        tap_rows.append(jnp.stack(across))
    return jnp.stack(tap_rows)


def input_grad(slope, kernel, stride, size_in):
    size_out = slope.shape[1]
    full_size = size_in + 2
    reach = stride * (size_out - 1) + 1
    summed = jnp.zeros((slope.shape[0], full_size, full_size, kernel.shape[2]), jnp.float32)
    for tap_row in range(3):
        for tap_col in range(3):
            term = jnp.einsum(
                "nhwo,co->nhwc", slope, kernel[tap_row, tap_col], preferred_element_type=jnp.float32
            )
            summed = summed + lax.pad(
                term,
                jnp.float32(0.0),
                (
                    (0, 0, 0),
                    (tap_row, full_size - tap_row - reach, stride - 1),
                    (tap_col, full_size - tap_col - reach, stride - 1),
                    (0, 0, 0),
                ),
            )
    return summed[:, 1:-1, 1:-1, :]


def proj_input_grad(slope, kernel, size_in):
    term = jnp.einsum("nhwo,co->nhwc", slope, kernel, preferred_element_type=jnp.float32)
    margin = size_in - 2 * slope.shape[1] + 1
    return lax.pad(term, jnp.float32(0.0), ((0, 0, 0), (0, margin, 1), (0, margin, 1), (0, 0, 0)))


def moments(values):
    return (jnp.sum(values, axis=(0, 1, 2)), jnp.sum(values * values, axis=(0, 1, 2)))


def normalize(values, total, square_total, number):
    center = total / number
    factor = lax.rsqrt(square_total / number - center * center + NORM_EPS)
    return ((values - center) * factor, factor)


def norm_back(upstream, normed, factor, gain, total, cross, number):
    return gain * factor * (upstream - total / number - normed * (cross / number))


def silu_slope(values):
    gate = jax.nn.sigmoid(values)
    return gate * (1.0 + values * (1.0 - gate))


def adamw_step(weight, gradient, first, second, rate, decay):
    first_new = BETA_ONE * first + (1.0 - BETA_ONE) * gradient
    second_new = BETA_TWO * second + (1.0 - BETA_TWO) * gradient * gradient
    first_hat = first_new / (1.0 - BETA_ONE**STEP)
    second_hat = second_new / (1.0 - BETA_TWO**STEP)
    updated = weight - rate * (first_hat / (jnp.sqrt(second_hat) + ADAM_EPS) + decay * weight)
    return (updated, first_new, second_new)


def body(
    image_big,
    image_small,
    slope_big,
    slope_small,
    conv1_weight,
    conv2_weight,
    proj_weight,
    norm_params,
    first_conv1,
    first_conv2,
    first_proj,
    first_norms,
    second_conv1,
    second_conv2,
    second_proj,
    second_norms,
):
    bfloat = jnp.bfloat16
    kernel_one, kernel_two, kernel_proj = (
        lax.all_gather(conv1_weight.astype(bfloat), "batch", axis=2, tiled=True),
        lax.all_gather(conv2_weight.astype(bfloat), "batch", axis=2, tiled=True),
        lax.all_gather(proj_weight.astype(bfloat), "batch", axis=0, tiled=True),
    )
    inputs_big, inputs_small = (
        lax.all_gather(image_big, "chan", axis=0, tiled=True),
        lax.all_gather(image_small, "chan", axis=0, tiled=True),
    )
    groups = (inputs_big, inputs_small)
    batch_width = lax.axis_size("batch")
    first_pre = [conv_taps(images, kernel_one, 2) for images in groups]
    numbers = [
        values.shape[0] * values.shape[1] * values.shape[2] * batch_width for values in first_pre
    ]
    sum_big, square_big = moments(first_pre[0])
    sum_small, square_small = moments(first_pre[1])
    sum_big, square_big, sum_small, square_small = lax.psum(
        (sum_big, square_big, sum_small, square_small), "batch"
    )
    first_norm = [
        normalize(first_pre[0], sum_big, square_big, numbers[0]),
        normalize(first_pre[1], sum_small, square_small, numbers[1]),
    ]
    shaped = [normed * norm_params[0] + norm_params[1] for normed, factor in first_norm]
    hidden = [jax.nn.silu(values).astype(bfloat) for values in shaped]
    hidden_big, hidden_small = (
        lax.all_gather(hidden[0], "chan", axis=3, tiled=True),
        lax.all_gather(hidden[1], "chan", axis=3, tiled=True),
    )
    hidden_full = (hidden_big, hidden_small)
    second_pre = [conv_taps(values, kernel_two, 1) for values in hidden_full]
    proj_pre = [
        jnp.einsum(
            "nhwc,co->nhwo", images[:, ::2, ::2, :], kernel_proj, preferred_element_type=jnp.float32
        )
        for images in groups
    ]
    two_big, two_sq_big = moments(second_pre[0])
    two_small, two_sq_small = moments(second_pre[1])
    side_big, side_sq_big = moments(proj_pre[0])
    side_small, side_sq_small = moments(proj_pre[1])
    (
        two_big,
        two_sq_big,
        two_small,
        two_sq_small,
        side_big,
        side_sq_big,
        side_small,
        side_sq_small,
    ) = lax.psum(
        (
            two_big,
            two_sq_big,
            two_small,
            two_sq_small,
            side_big,
            side_sq_big,
            side_small,
            side_sq_small,
        ),
        "batch",
    )
    second_norm = [
        normalize(second_pre[0], two_big, two_sq_big, numbers[0]),
        normalize(second_pre[1], two_small, two_sq_small, numbers[1]),
    ]
    proj_norm = [
        normalize(proj_pre[0], side_big, side_sq_big, numbers[0]),
        normalize(proj_pre[1], side_small, side_sq_small, numbers[1]),
    ]
    summed = [
        second_norm[which][0] * norm_params[2]
        + norm_params[3]
        + proj_norm[which][0] * norm_params[4]
        + norm_params[5]
        for which in range(2)
    ]
    out_big = jax.nn.silu(summed[0]).astype(bfloat)
    out_small = jax.nn.silu(summed[1]).astype(bfloat)
    slopes = (slope_big, slope_small)
    upstream = [slopes[which].astype(jnp.float32) * silu_slope(summed[which]) for which in range(2)]
    outer_big = jnp.sum(upstream[0], axis=(0, 1, 2))
    cross_two_big = jnp.sum(upstream[0] * second_norm[0][0], axis=(0, 1, 2))
    cross_side_big = jnp.sum(upstream[0] * proj_norm[0][0], axis=(0, 1, 2))
    outer_small = jnp.sum(upstream[1], axis=(0, 1, 2))
    cross_two_small = jnp.sum(upstream[1] * second_norm[1][0], axis=(0, 1, 2))
    cross_side_small = jnp.sum(upstream[1] * proj_norm[1][0], axis=(0, 1, 2))
    outer_big, cross_two_big, cross_side_big, outer_small, cross_two_small, cross_side_small = (
        lax.psum(
            (
                outer_big,
                cross_two_big,
                cross_side_big,
                outer_small,
                cross_two_small,
                cross_side_small,
            ),
            "batch",
        )
    )
    outer_sums = (outer_big, outer_small)
    cross_two = (cross_two_big, cross_two_small)
    cross_side = (cross_side_big, cross_side_small)
    slope_two = [
        norm_back(
            upstream[which],
            second_norm[which][0],
            second_norm[which][1],
            norm_params[2],
            outer_sums[which],
            cross_two[which],
            numbers[which],
        ).astype(bfloat)
        for which in range(2)
    ]
    slope_proj = [
        norm_back(
            upstream[which],
            proj_norm[which][0],
            proj_norm[which][1],
            norm_params[4],
            outer_sums[which],
            cross_side[which],
            numbers[which],
        ).astype(bfloat)
        for which in range(2)
    ]
    part_big = input_grad(slope_two[0], kernel_two, 1, hidden_big.shape[1])
    part_small = input_grad(slope_two[1], kernel_two, 1, hidden_small.shape[1])
    back_big, back_small = (
        lax.psum_scatter(part_big, "chan", scatter_dimension=3, tiled=True),
        lax.psum_scatter(part_small, "chan", scatter_dimension=3, tiled=True),
    )
    inner = [back_big * silu_slope(shaped[0]), back_small * silu_slope(shaped[1])]
    inner_big = jnp.sum(inner[0], axis=(0, 1, 2))
    cross_one_big = jnp.sum(inner[0] * first_norm[0][0], axis=(0, 1, 2))
    inner_small = jnp.sum(inner[1], axis=(0, 1, 2))
    cross_one_small = jnp.sum(inner[1] * first_norm[1][0], axis=(0, 1, 2))
    inner_big, cross_one_big, inner_small, cross_one_small = lax.psum(
        (inner_big, cross_one_big, inner_small, cross_one_small), "batch"
    )
    inner_sums = (inner_big, inner_small)
    cross_one = (cross_one_big, cross_one_small)
    slope_one = [
        norm_back(
            inner[which],
            first_norm[which][0],
            first_norm[which][1],
            norm_params[0],
            inner_sums[which],
            cross_one[which],
            numbers[which],
        ).astype(bfloat)
        for which in range(2)
    ]
    size_big = image_big.shape[1]
    size_small = image_small.shape[1]
    input_part_big = input_grad(slope_one[0], kernel_one, 2, size_big) + proj_input_grad(
        slope_proj[0], kernel_proj, size_big
    )
    input_part_small = input_grad(slope_one[1], kernel_one, 2, size_small) + proj_input_grad(
        slope_proj[1], kernel_proj, size_small
    )
    grad_big, grad_small = (
        lax.psum_scatter(input_part_big, "chan", scatter_dimension=0, tiled=True),
        lax.psum_scatter(input_part_small, "chan", scatter_dimension=0, tiled=True),
    )
    part_conv1 = kernel_grad(groups[0], slope_one[0], 2) + kernel_grad(groups[1], slope_one[1], 2)
    part_conv2 = kernel_grad(hidden_full[0], slope_two[0], 1) + kernel_grad(
        hidden_full[1], slope_two[1], 1
    )
    part_proj = jnp.einsum(
        "nhwc,nhwo->co",
        groups[0][:, ::2, ::2, :],
        slope_proj[0],
        preferred_element_type=jnp.float32,
    ) + jnp.einsum(
        "nhwc,nhwo->co",
        groups[1][:, ::2, ::2, :],
        slope_proj[1],
        preferred_element_type=jnp.float32,
    )
    grad_conv1, grad_conv2, grad_proj = (
        lax.psum_scatter(part_conv1, "batch", scatter_dimension=2, tiled=True),
        lax.psum_scatter(part_conv2, "batch", scatter_dimension=2, tiled=True),
        lax.psum_scatter(part_proj, "batch", scatter_dimension=0, tiled=True),
    )
    grad_norms = jnp.stack(
        [
            cross_one_big + cross_one_small,
            inner_big + inner_small,
            cross_two_big + cross_two_small,
            outer_big + outer_small,
            cross_side_big + cross_side_small,
            outer_big + outer_small,
        ]
    )
    new_conv1, moment_conv1, square_conv1 = adamw_step(
        conv1_weight, grad_conv1, first_conv1, second_conv1, (9.0 * C_IN) ** (-0.5), DECAY
    )
    new_conv2, moment_conv2, square_conv2 = adamw_step(
        conv2_weight, grad_conv2, first_conv2, second_conv2, (9.0 * C_OUT) ** (-0.5), DECAY
    )
    new_proj, moment_proj, square_proj = adamw_step(
        proj_weight, grad_proj, first_proj, second_proj, (1.0 * C_IN) ** (-0.5), DECAY
    )
    new_norms, moment_norms, square_norms = adamw_step(
        norm_params, grad_norms, first_norms, second_norms, NORM_RATE, 0.0
    )
    return (
        out_big,
        out_small,
        grad_big.astype(bfloat),
        grad_small.astype(bfloat),
        grad_conv1,
        grad_conv2,
        grad_proj,
        grad_norms,
        new_conv1,
        new_conv2,
        new_proj,
        new_norms,
        moment_conv1,
        moment_conv2,
        moment_proj,
        moment_norms,
        square_conv1,
        square_conv2,
        square_proj,
        square_norms,
    )


def solution(mesh):
    placed = (
        P(("batch", "chan"), None, None, None),
        P(("batch", "chan"), None, None, None),
        P("batch", None, None, "chan"),
        P("batch", None, None, "chan"),
        P(None, None, "batch", "chan"),
        P(None, None, "batch", "chan"),
        P("batch", "chan"),
        P(None, "chan"),
        P(None, None, "batch", "chan"),
        P(None, None, "batch", "chan"),
        P("batch", "chan"),
        P(None, "chan"),
        P(None, None, "batch", "chan"),
        P(None, None, "batch", "chan"),
        P("batch", "chan"),
        P(None, "chan"),
    )
    return jax.shard_map(
        body,
        mesh=mesh,
        in_specs=placed,
        out_specs=(
            P("batch", None, None, "chan"),
            P("batch", None, None, "chan"),
            P(("batch", "chan"), None, None, None),
            P(("batch", "chan"), None, None, None),
            P(None, None, "batch", "chan"),
            P(None, None, "batch", "chan"),
            P("batch", "chan"),
            P(None, "chan"),
            P(None, None, "batch", "chan"),
            P(None, None, "batch", "chan"),
            P("batch", "chan"),
            P(None, "chan"),
            P(None, None, "batch", "chan"),
            P(None, None, "batch", "chan"),
            P("batch", "chan"),
            P(None, "chan"),
            P(None, None, "batch", "chan"),
            P(None, None, "batch", "chan"),
            P("batch", "chan"),
            P(None, "chan"),
        ),
        check_vma=False,
    )
```

profile of v0, /device:TPU:0, one launch (start us, length us, event | category | flops | bytes accessed | tf_op | source)
XLA Modules:
  0.0 1332.7 jit_solution(5456838402609253158)
XLA Ops:
  21.6 41.2 %all-gather.12.cloned.1.call-done = bf16[128,6,6,256]{3,0,2,1:T(8,128)(2,1)} async-done(((bf16[32,6,6,256]{3,0,2,1:T(8,128)(2,1)}), bf16[128,6,6,256]{3,0,2,1:T(8,128)(2,1)}) %all-gather.12.cloned.1.call-update) | async-done | bytes 2359312 | tf_op jit(solution)/shard_map/all_gather | solution.py:143
  67.7 113.1 %all-gather.6.cloned.1.call-done = bf16[64,14,14,256]{3,0,2,1:T(8,128)(2,1)} async-done(((bf16[16,14,14,256]{3,0,2,1:T(8,128)(2,1)}), bf16[64,14,14,256]{3,0,2,1:T(8,128)(2,1)}) %all-gather.6.cloned.1.call-update) | async-done | bytes 6422544 | tf_op jit(solution)/shard_map/all_gather | solution.py:142
  190.5 14.2 %all-reduce.45 = (f32[128]{0:T(128)S(1)}, f32[128]{0:T(128)S(1)}, f32[128]{0:T(128)S(1)}, f32[128]{0:T(128)S(1)}) all-reduce(f32[128]{0:T(128)} %get-tuple-element.88, f32[128]{0:T(128)} %get-tuple-element.87, f32[128]{0:T(128)} %get-tuple-element.99, f32[128]{0:T(128)S(1)} %get-tuple-element.98), channel_id=1, replica_groups=mesh['batch'=8,'chan'=4] {'batch'}, use_global_device_ids=true, to_apply=%region_3.4 | all-reduce | flops 512 | bytes 4096 | tf_op jit(solution)/shard_map/psum | solution.py:153
  223.1 16.3 %all-gather.14.cloned.1.call-done = bf16[128,3,3,512]{3,0,2,1:T(8,128)(2,1)} async-done(((bf16[128,3,3,128]{3,0,2,1:T(8,128)(2,1)}), bf16[128,3,3,512]{3,0,2,1:T(8,128)(2,1)}) %all-gather.14.cloned.1.call-update) | async-done | bytes 1179664 | tf_op jit(solution)/shard_map/all_gather | solution.py:164
  247.1 57.1 %all-gather.8.cloned.1.call-done = bf16[64,7,7,512]{3,0,2,1:T(8,128)(2,1)} async-done(((bf16[64,7,7,128]{3,0,2,1:T(8,128)(2,1)}), bf16[64,7,7,512]{3,0,2,1:T(8,128)(2,1)}) %all-gather.8.cloned.1.call-update) | async-done | bytes 3211280 | tf_op jit(solution)/shard_map/all_gather | solution.py:163
  317.2 14.5 %all-reduce.44 = (f32[128]{0:T(128)}, f32[128]{0:T(128)}, f32[128]{0:T(128)}, f32[128]{0:T(128)}, f32[128]{0:T(128)}, /*index=5*/f32[128]{0:T(128)}, f32[128]{0:T(128)}, f32[128]{0:T(128)}) all-reduce(f32[128]{0:T(128)} %get-tuple-element.90, f32[128]{0:T(128)} %get-tuple-element.89, ...), channel_id=1, replica_groups=mesh['batch'=8,'chan'=4] {'batch'}, use_global_device_ids=true, to_apply=%region_11.12 | all-reduce | flops 1024 | bytes 8192 | tf_op jit(solution)/shard_map/psum | solution.py:187
  422.4 19.1 %slice_add_fusion.1 = f32[64,7,7,512]{3,0,2,1:T(8,128)} fusion(f32[64,9,9,512]{3,0,2,1:T(8,128)} %fusion.64, f32[64,9,9,512]{3,0,2,1:T(8,128)} %fusion.61, f32[64,7,7,512]{3,0,2,1:T(8,128)} %fusion.58, f32[64,9,9,512]{3,0,2,1:T(8,128)} %fusion.55, f32[64,9,9,512]{3,0,2,1:T(8,128)} %fusion.52, f32[64,7,7,512]{3,0,2,1:T(8,128)} %fusion.49, ...), kind=kLoop, calls=%fused_computation.29 | loop fusion | flops 9633792 | bytes 51380224 | tf_op jit(solution)/shard_map/add | solution.py:70
  464.1 86.8 %reduce-scatter.10.cloned.1.call-done = f32[64,7,7,128]{3,0,2,1:T(8,128)} async-done(((f32[64,7,7,512]{3,0,2,1:T(8,128)}), f32[64,7,7,128]{3,0,2,1:T(8,128)}) %reduce-scatter.10.cloned.1.call-update) | async-done | bytes 1605648 | tf_op jit(solution)/shard_map/reduce_scatter | solution.py:268
  554.8 13.7 %all-reduce.42 = (f32[128]{0:T(128)S(1)}, f32[128]{0:T(128)S(1)}, f32[128]{0:T(128)S(1)}, f32[128]{0:T(128)S(1)}, f32[128]{0:T(128)S(1)}, /*index=5*/f32[128]{0:T(128)S(1)}) all-reduce(f32[128]{0:T(128)S(1)} %copy-done.84, f32[128]{0:T(128)S(1)} %get-tuple-element.81, ...), channel_id=1, replica_groups=mesh['batch'=8,'chan'=4] {'batch'}, use_global_device_ids=true, to_apply=%region_34.35 | all-reduce | flops 768 | bytes 6144 | tf_op jit(solution)/shard_map/psum | solution.py:226
  685.0 30.8 %pad.147 = f32[64,16,16,256]{3,0,2,1:T(8,128)} pad(f32[64,7,7,256]{3,0,2,1:T(8,128)} %fusion.72, f32[]{:T(128)} %constant.65.clone.1), padding=0_0_0x0_3_1x0_3_1x0_0_0 | pad | bytes 19988484 | tf_op jit(solution)/shard_map/pad | solution.py:70
  715.8 30.8 %pad.148 = f32[64,16,16,256]{3,0,2,1:T(8,128)} pad(f32[64,7,7,256]{3,0,2,1:T(8,128)} %fusion.75, f32[]{:T(128)} %constant.65.clone.1), padding=0_0_0x0_3_1x1_2_1x0_0_0 | pad | bytes 19988484 | tf_op jit(solution)/shard_map/pad | solution.py:70
  746.7 30.8 %pad.149 = f32[64,16,16,256]{3,0,2,1:T(8,128)} pad(f32[64,7,7,256]{3,0,2,1:T(8,128)} %fusion.77, f32[]{:T(128)} %constant.65.clone.1), padding=0_0_0x0_3_1x2_1_1x0_0_0 | pad | bytes 19988484 | tf_op jit(solution)/shard_map/pad | solution.py:70
  777.5 30.0 %pad.360 = f32[64,14,15,256]{3,0,2,1:T(8,128)} pad(f32[64,7,7,256]{3,0,2,1:T(8,128)} %fusion.85, f32[]{:T(128)} %constant.65.clone.1), padding=0_0_0x1_0_1x0_2_1x0_0_0 | pad | bytes 16973828
  807.5 29.9 %pad.361 = f32[64,14,15,256]{3,0,2,1:T(8,128)} pad(f32[64,7,7,256]{3,0,2,1:T(8,128)} %fusion.79, f32[]{:T(128)} %constant.65.clone.1), padding=0_0_0x0_1_1x0_2_1x0_0_0 | pad | bytes 16973828
  837.4 29.7 %pad.227 = f32[64,14,14,256]{3,0,2,1:T(8,128)} pad(f32[64,7,7,256]{3,0,2,1:T(8,128)} %fusion.81, f32[]{:T(128)} %constant.65.clone.1), padding=0_0_0x0_1_1x0_1_1x0_0_0 | pad | bytes 16056324 | tf_op jit(solution)/shard_map/slice | solution.py:80
  867.2 29.6 %pad.228 = f32[64,14,14,256]{3,0,2,1:T(8,128)} pad(f32[64,7,7,256]{3,0,2,1:T(8,128)} %fusion.83, f32[]{:T(128)} %constant.65.clone.1), padding=0_0_0x0_1_1x1_0_1x0_0_0 | pad | bytes 16056324 | tf_op jit(solution)/shard_map/slice | solution.py:80
  896.8 29.6 %pad.230 = f32[64,14,14,256]{3,0,2,1:T(8,128)} pad(f32[64,7,7,256]{3,0,2,1:T(8,128)} %fusion.87, f32[]{:T(128)} %constant.65.clone.1), padding=0_0_0x1_0_1x0_1_1x0_0_0 | pad | bytes 16056324 | tf_op jit(solution)/shard_map/slice | solution.py:80
  926.4 29.8 %pad.231 = f32[64,14,14,256]{3,0,2,1:T(8,128)} pad(f32[64,7,7,256]{3,0,2,1:T(8,128)} %fusion.89, f32[]{:T(128)} %constant.65.clone.1), padding=0_0_0x1_0_1x1_0_1x0_0_0 | pad | bytes 16056324 | tf_op jit(solution)/shard_map/slice | solution.py:80
  957.7 13.4 %add_add_fusion.1 = f32[128,8,8,256]{3,0,2,1:T(8,128)} fusion(f32[128,8,8,256]{3,0,2,1:T(8,128)} %pad.168, f32[128,8,8,256]{3,0,2,1:T(8,128)} %pad.166, f32[128,8,8,256]{3,0,2,1:T(8,128)} %pad.167), kind=kLoop, calls=%fused_computation.9 | loop fusion | flops 4194304 | bytes 33554432 | tf_op jit(solution)/shard_map/add | solution.py:70
  973.3 29.6 %pad.156 = f32[64,14,14,256]{3,0,2,1:T(8,128)} pad(f32[64,7,7,256]{3,0,2,1:T(8,128)} %fusion.67, f32[]{:T(128)} %constant.65.clone.1), padding=0_0_0x0_1_1x0_1_1x0_0_0 | pad | bytes 16056324 | tf_op jit(solution)/shard_map/pad | solution.py:86
  1003.0 16.1 %fusion.11 = f32[128,6,6,256]{3,0,2,1:T(8,128)} fusion(f32[128,6,6,256]{3,0,2,1:T(8,128)} %pad.175, f32[128,6,6,256]{3,0,2,1:T(8,128)} %pad.239, f32[128,6,6,256]{3,0,2,1:T(8,128)} %pad.238, f32[128,6,6,256]{3,0,2,1:T(8,128)} %pad.236, f32[128,6,6,256]{3,0,2,1:T(8,128)} %pad.235, f32[128,8,8,256]{3,0,2,1:T(8,128)} %add_add_fusion.1, ...), kind=kLoop, calls=%fused_computation.41 | loop fusion | flops 8257536 | bytes 42467328 | tf_op jit(solution)/shard_map/add | solution.py:298
  1019.1 24.7 %add_add_fusion = f32[64,16,16,256]{3,0,2,1:T(8,128)} fusion(f32[64,16,16,256]{3,0,2,1:T(8,128)} %pad.149, f32[64,16,16,256]{3,0,2,1:T(8,128)} %pad.147, f32[64,16,16,256]{3,0,2,1:T(8,128)} %pad.148), kind=kLoop, calls=%fused_computation | loop fusion | flops 8388608 | bytes 67108864 | tf_op jit(solution)/shard_map/add | solution.py:70
  1043.8 39.4 %fusion.5 = f32[64,14,14,256]{3,0,2,1:T(8,128)} fusion(f32[64,14,14,256]{3,0,2,1:T(8,128)} %pad.156, f32[64,14,14,256]{3,0,2,1:T(8,128)} %pad.231, f32[64,14,14,256]{3,0,2,1:T(8,128)} %pad.230, f32[64,14,14,256]{3,0,2,1:T(8,128)} %pad.228, f32[64,14,14,256]{3,0,2,1:T(8,128)} %pad.227, f32[64,16,16,256]{3,0,2,1:T(8,128)} %add_add_fusion, ...), kind=kLoop, calls=%fused_computation.7 | loop fusion | flops 22478848 | bytes 115605504 | tf_op jit(solution)/shard_map/add | solution.py:295
  1105.5 216.8 %reduce-scatter.12.cloned.1.call-done = f32[16,14,14,256]{3,0,2,1:T(8,128)} async-done(((f32[64,14,14,256]{3,0,2,1:T(8,128)}), f32[16,14,14,256]{3,0,2,1:T(8,128)}) %reduce-scatter.12.cloned.1.call-update) | async-done | bytes 3211280 | tf_op jit(solution)/shard_map/reduce_scatter | solution.py:302
  (404 shorter events, 329.8 us)
Async XLA Ops:
  7.2 55.6 %all-gather.12.cloned.1.call-start = ((), (), s32[]{:S(2)}) async-start(), calls=%async_computation.10 | async-start | bytes 2949120 | tf_op jit(solution)/shard_map/all_gather | solution.py:143
  8.0 172.8 %all-gather.6.cloned.1.call-start = ((), (), s32[]{:S(2)}) async-start(), calls=%async_computation.7 | async-start | bytes 8028160 | tf_op jit(solution)/shard_map/all_gather | solution.py:142
  8.7 214.3 %all-gather.10.cloned.1.call-start = ((), (), s32[]{:S(2)}) async-start(), calls=%async_computation.9 | async-start | bytes 1327104 | tf_op jit(solution)/shard_map/all_gather | solution.py:138
  9.5 229.8 %all-gather.14.cloned.1.call-start = ((), (), s32[]{:S(2)}) async-start(), calls=%async_computation.11 | async-start | bytes 1474560 | tf_op jit(solution)/shard_map/all_gather | solution.py:164
  21.0 166.9 %copy-start.13 = (bf16[3,3,256,128]{3,2,1,0:T(8,128)(2,1)}, bf16[3,3,256,128]{3,2,1,0:T(8,128)(2,1)S(1)}, u32[]{:S(2)}) copy-start(bf16[3,3,256,128]{3,2,1,0:T(8,128)(2,1)S(1)} %all_gather.22) | copy-start | bytes 1769476
  67.7 137.0 %copy-start.18 = (f32[128,3,3,128]{3,0,2,1:T(8,128)}, f32[128,3,3,128]{3,0,2,1:T(8,128)S(1)}, u32[]{:S(2)}) copy-start(f32[128,3,3,128]{3,0,2,1:T(8,128)S(1)} %get-tuple-element.190) | copy-start | bytes 1769476
  206.1 98.1 %all-gather.8.cloned.1.call-start = ((), (), s32[]{:S(2)}) async-start(), calls=%async_computation.8 | async-start | bytes 4014080 | tf_op jit(solution)/shard_map/all_gather | solution.py:163
  209.1 251.9 %reduce-scatter.14.cloned.1.call-start = ((), (), s32[]{:S(2)}) async-start(), calls=%async_computation.14 | async-start | bytes 2949120 | tf_op jit(solution)/shard_map/reduce_scatter | solution.py:269
  381.3 169.6 %reduce-scatter.10.cloned.1.call-start = ((), (), s32[]{:S(2)}) async-start(), calls=%async_computation.12 | async-start | bytes 8028160 | tf_op jit(solution)/shard_map/reduce_scatter | solution.py:268
  383.8 33.0 %copy-start.5 = (bf16[64,7,7,128]{3,0,2,1:T(8,128)(2,1)}, bf16[64,7,7,128]{3,0,2,1:T(8,128)(2,1)S(1)}, u32[]{:S(2)}) copy-start(bf16[64,7,7,128]{3,0,2,1:T(8,128)(2,1)S(1)} %multiply_convert_fusion.2) | copy-start | bytes 2408452
  441.5 641.9 %reduce-scatter.20.cloned.1.call-start = ((), (), s32[]{:S(2)}) async-start(), calls=%async_computation.17 | async-start | bytes 2654208 | tf_op jit(solution)/shard_map/reduce_scatter | solution.py:322
  460.8 90.1 %copy-start.64 = (f32[128]{0:T(128)S(1)}, f32[128]{0:T(128)}, u32[]{:S(2)}) copy-start(f32[128]{0:T(128)} %copy-done.63) | copy-start | bytes 1540
  460.8 90.1 %copy-start.66 = (f32[128]{0:T(128)S(1)}, f32[128]{0:T(128)}, u32[]{:S(2)}) copy-start(f32[128]{0:T(128)} %copy-done.65) | copy-start | bytes 1540
  460.9 626.2 %reduce-scatter.22.cloned.1.call-start = ((), (), s32[]{:S(2)}) async-start(), calls=%async_computation.18 | async-start | bytes 147456
  464.1 90.7 %copy-start.83 = (f32[128]{0:T(128)S(1)}, f32[128]{0:T(128)}, u32[]{:S(2)}) copy-start(f32[128]{0:T(128)} %get-tuple-element.94) | copy-start | bytes 1540
  464.1 90.7 %copy-start.84 = (f32[128]{0:T(128)S(1)}, f32[128]{0:T(128)}, u32[]{:S(2)}) copy-start(f32[128]{0:T(128)} %get-tuple-element.83) | copy-start | bytes 1540
  464.1 105.4 %copy-start.90 = (f32[128]{0:T(128)S(1)}, f32[128]{0:T(128)}, u32[]{:S(2)}) copy-start(f32[128]{0:T(128)} %get-tuple-element.153) | copy-start | bytes 1540
  464.1 106.8 %copy-start.14 = (bf16[3,3,256,128]{3,2,1,0:T(8,128)(2,1)S(1)}, bf16[3,3,256,128]{3,2,1,0:T(8,128)(2,1)}, u32[]{:S(2)}) copy-start(bf16[3,3,256,128]{3,2,1,0:T(8,128)(2,1)} %copy-done.13) | copy-start | bytes 1769476
  612.7 475.7 %reduce-scatter.18.cloned.1.call-start = ((), (), s32[]{:S(2)}) async-start(), calls=%async_computation.16 | async-start | bytes 1327104 | tf_op jit(solution)/shard_map/reduce_scatter | solution.py:321
  926.4 29.8 %copy-start.40 = (f32[1,3,256,128]{3,2,1,0:T(8,128)S(1)}, f32[1,3,256,128]{3,2,1,0:T(8,128)}, u32[]{:S(2)}) copy-start(f32[1,3,256,128]{3,2,1,0:T(8,128)} %maximum_bitcast_fusion.7) | copy-start | bytes 1179652
  926.4 29.8 %copy-start.41 = (f32[1,3,256,128]{3,2,1,0:T(8,128)S(1)}, f32[1,3,256,128]{3,2,1,0:T(8,128)}, u32[]{:S(2)}) copy-start(f32[1,3,256,128]{3,2,1,0:T(8,128)} %maximum_bitcast_fusion.8) | copy-start | bytes 1179652
  957.4 145.9 %reduce-scatter.16.cloned.1.call-start = ((), (), s32[]{:S(2)}) async-start(), calls=%async_computation.15 | async-start | bytes 5898240 | tf_op jit(solution)/shard_map/reduce_scatter | solution.py:303
  1019.1 303.2 %reduce-scatter.12.cloned.1.call-start = ((), (), s32[]{:S(2)}) async-start(), calls=%async_computation.13 | async-start | bytes 16056320 | tf_op jit(solution)/shard_map/reduce_scatter | solution.py:302
  1086.5 239.1 %copy-start.60 = (f32[6,128]{1,0:T(8,128)}, f32[6,128]{1,0:T(8,128)S(1)}, u32[]{:S(2)}) copy-start(f32[6,128]{1,0:T(8,128)S(1)} %stack.280) | copy-start | bytes 9220
  (87 other events, 441.2 us)
Sparse Core Ops, SparseCore 0:
  9.6 53.1 all-gather.11
  64.4 116.3 all-gather.5
  183.2 22.3 all-gather.9
  207.6 31.6 all-gather.13
  241.3 62.8 all-gather.7
  381.5 44.3 reduce-scatter.13
  441.6 109.2 reduce-scatter.9
  554.9 42.9 reduce-scatter.19
  612.8 32.1 reduce-scatter.21
  957.5 35.5 reduce-scatter.17
  1019.2 84.0 reduce-scatter.15
  1105.6 216.5 reduce-scatter.11
where the time goes:
time: 1360 us; the launch traced here: 1330 us
  waiting for transfers between devices  546 us (40%)
  local copies, waits for them, and re-layouts  367 us (27%)
  other arithmetic  180 us (13%)
  matrix products  148 us (11%)
  blocking collectives  74.6 us (5%)
  between operations  15.9 us (1%)
    reduce_scatter x1, waiting for transfers between devices, body(): lax.psum_scatter(input_part_big, 'chan', scatter_dimension=0, tiled=True)  217 us
    slice x8, local copies, waits for them, and re-layouts, input_grad(): return summed[:, 1:-1, 1:-1, :]  140 us
    all_gather x1, waiting for transfers between devices, body(): lax.all_gather(image_big, 'chan', axis=0, tiled=True)  113 us
    pad x6, local copies, waits for them, and re-layouts, input_grad(): lax.pad(term, jnp.float32(0.0), ((0, 0, 0), (tap_row, full_size - tap_row...  112 us
    reduce_scatter x1, waiting for transfers between devices, body(): lax.psum_scatter(part_big, 'chan', scatter_dimension=3, tiled=True)  86.8 us
    unnamed x203, local copies, waits for them, and re-layouts  78.8 us
    add x6, other arithmetic, input_grad(): summed + lax.pad(term, jnp.float32(0.0), ((0, 0, 0), (tap_row, full_size...  73.5 us
    all_gather x1, waiting for transfers between devices, body(): lax.all_gather(hidden[0], 'chan', axis=3, tiled=True)  57.1 us
  transfers between devices with their start and end apart: 12, of which 7 were waited for; matrix products, arithmetic and copies ran while one was open for 48% of the time, Pallas kernels for 0%

commit v1 on v0

--- a/solution.py
+++ b/solution.py
@@ -1,19 +1,561 @@
+import functools
+
 import jax
 import jax.numpy as jnp
 from jax import lax
+from jax.experimental import pallas as pl
+from jax.experimental.pallas import tpu as pltpu
 from jax.sharding import PartitionSpec as P
 
 C_IN = 256
 C_OUT = 512
 STEP = 5
-
-
 NORM_EPS = 1e-05
 BETA_ONE = 0.5
 BETA_TWO = 0.5
 ADAM_EPS = 1e-08
 DECAY = 0.01
 NORM_RATE = 0.3
+MESH = pl.DeviceIdType.MESH
+BF16 = jnp.bfloat16
+F32 = jnp.float32
+COPIES = 176
+VMEM_BYTES = 60 << 20
+
+
+def silu_slope(values):
+    gate = jax.nn.sigmoid(values)
+    return gate * (1.0 + values * (1.0 - gate))
+
+
+def adamw_step(weight, gradient, first, second, rate, decay):
+    first_new = BETA_ONE * first + (1.0 - BETA_ONE) * gradient
+    second_new = BETA_TWO * second + (1.0 - BETA_TWO) * gradient * gradient
+    first_hat = first_new / (1.0 - BETA_ONE**STEP)
+    second_hat = second_new / (1.0 - BETA_TWO**STEP)
+    updated = weight - rate * (first_hat / (jnp.sqrt(second_hat) + ADAM_EPS) + decay * weight)
+    return (updated, first_new, second_new)
+
+
+def fold(values):
+    rows, channels = values.shape
+    return jnp.sum(values.reshape(rows // 8, 8, channels), axis=0)
+
+
+def block_kernel(
+    cfg,
+    img_big, img_small, slo_big, slo_small, w1_in, w2_in, wp_in, norms_in,
+    out_big, out_small, grad_big, grad_small, grad_one, grad_two, grad_norms,
+    w1, w2, x_big, x_small, h_big, h_small, first_pre, second_pre, proj_pre, work,
+    sl_big, sl_small, os_big, os_small, t_big, t_small, p_big, p_small, s_big, s_small,
+    norms, norm_rows, stat_a, stat_b, a1, r1, rx1, ry1, rxx1, ryy1, c1, rz1,
+    a2, r2, rx2, ry2, rxx2, ryy2, c2, rz2,
+    send_sem, recv_sem, local_sem,
+):
+    nb_img, ns_img, ob, os_, number_big, number_small = cfg
+    rows_b, rows_s = ob * ob * nb_img, os_ * os_ * ns_img
+    step_b, step_s = ob * nb_img, os_ * ns_img
+    b = lax.axis_index("batch")
+    z = lax.axis_index("chan")
+    core = lax.rem(b, 2)
+    x = lax.rem(lax.div(b, 2), 2)
+    y = lax.div(b, 4)
+    x_peer = (b + 2 - 4 * x, z)
+    y_peer = (b + 4 - 8 * y, z)
+    sibling = (b + 1 - 2 * core, z)
+    z_peers = [(b, lax.rem(z + d, 4)) for d in (1, 2, 3)]
+    b_peers = [(lax.rem(b + d, 8), z) for d in range(1, 8)]
+    lanes = lambda which: pl.ds(pl.multiple_of(which * 128, 128), 128)
+    mine = lanes(z)
+
+    used = [0]
+    started = []
+
+    def send(src, dst, peer):
+        slot = used[0]
+        used[0] += 1
+        copy = pltpu.make_async_remote_copy(
+            src_ref=src,
+            dst_ref=dst,
+            send_sem=send_sem.at[slot],
+            recv_sem=recv_sem.at[slot],
+            device_id=peer,
+            device_id_type=MESH,
+        )
+        copy.start()
+        started.append(copy)
+        return copy
+
+    barrier = pltpu.get_barrier_semaphore()
+    for peer in b_peers + z_peers:
+        pl.semaphore_signal(barrier, inc=1, device_id=peer, device_id_type=MESH)
+
+    loads = []
+
+    def load(src, dst):
+        copy = pltpu.make_async_copy(src, dst, local_sem.at[len(loads)])
+        copy.start()
+        loads.append(copy)
+
+    for hp in range(2):
+        for wp in range(2):
+            load(img_big.at[:, hp, :, wp], x_big.at[hp, wp, pl.ds(hp, ob), pl.ds(wp, ob)])
+            load(img_small.at[:, hp, :, wp], x_small.at[hp, wp, pl.ds(hp, os_), pl.ds(wp, os_)])
+    load(
+        slo_big.at[:, :, pl.ds(pl.multiple_of(z * nb_img, nb_img), nb_img)],
+        sl_big.at[:, :, :, mine],
+    )
+    load(
+        slo_small.at[:, :, pl.ds(pl.multiple_of(z * ns_img, ns_img), ns_img)],
+        sl_small.at[:, :, :, mine],
+    )
+    w1[0:9, y, x, core, :, mine] = w1_in[...].astype(BF16)
+    w1[9, y, x, core, :, mine] = wp_in[...].astype(BF16)
+    w2[:, y, x, core, :, mine] = w2_in[...].astype(BF16)
+    norms[z, 0:6] = norms_in[...]
+
+    pl.semaphore_wait(barrier, 10)
+
+    def gather_z(w):
+        piece = w.at[:, y, x, core, :, mine]
+        return [send(piece, piece, peer) for peer in z_peers]
+
+    def gather_xy(w):
+        piece = w.at[:, y, x, core]
+        return [
+            send(piece, piece, x_peer),
+            send(piece, piece, y_peer),
+            send(piece, piece, sibling),
+        ]
+
+    def gather_forward(w, near):
+        near[0].wait_recv()
+        piece = w.at[:, y, 1 - x, core]
+        part = w.at[:, y, 1 - x, core, :, pl.ds(0, 256)]
+        far_a = send(part, part, y_peer)
+        sib_x = send(piece, piece, sibling)
+        near[1].wait_recv()
+        piece = w.at[:, 1 - y, x, core]
+        part = w.at[:, 1 - y, x, core, :, pl.ds(256, 256)]
+        far_b = send(part, part, x_peer)
+        sib_y = send(piece, piece, sibling)
+        return [far_a, far_b, near[2], sib_x, sib_y]
+
+    def gather_last(w, far):
+        far[0].wait_recv()
+        far[1].wait_recv()
+        piece = w.at[:, 1 - y, 1 - x, core]
+        return far[2:] + [send(piece, piece, sibling)]
+
+    def finish(copies):
+        for copy in copies:
+            copy.wait_recv()
+
+    z_one = gather_z(w1)
+    z_norms = [send(norms.at[z], norms.at[z], peer) for peer in z_peers]
+    z_two = gather_z(w2)
+
+    zero = functools.partial(jnp.zeros, dtype=BF16)
+    for wp in range(2):
+        x_big[1, wp, 0] = zero((ob + 1, nb_img, 256))
+        x_small[1, wp, 0] = zero((os_ + 1, ns_img, 256))
+    for hp in range(2):
+        x_big[hp, 1, :, 0] = zero((ob + 1, nb_img, 256))
+        x_small[hp, 1, :, 0] = zero((os_ + 1, ns_img, 256))
+    for ref, side, images in (
+        (h_big, ob, nb_img), (t_big, ob, nb_img), (h_small, os_, ns_img), (t_small, os_, ns_img),
+    ):
+        ref[0] = zero((side + 2, images, 512))
+        ref[side + 1] = zero((side + 2, images, 512))
+        ref[:, 0] = zero((side + 2, images, 512))
+        ref[:, side + 1] = zero((side + 2, images, 512))
+    for ref, side, images in ((s_big, ob, nb_img), (s_small, os_, ns_img)):
+        ref[side] = zero((side + 1, images, 512))
+        ref[:, side] = zero((side + 1, images, 512))
+
+    finish(z_one)
+    near_one = gather_xy(w1)
+    finish(z_two)
+    near_two = gather_xy(w2)
+    slope_copies = []
+    for d in (1, 2, 3):
+        to = lax.rem(z + d, 4)
+        slope_copies.append(
+            send(
+                slo_big.at[:, :, pl.ds(pl.multiple_of(to * nb_img, nb_img), nb_img)],
+                sl_big.at[:, :, :, mine],
+                (b, to),
+            )
+        )
+        slope_copies.append(
+            send(
+                slo_small.at[:, :, pl.ds(pl.multiple_of(to * ns_img, ns_img), ns_img)],
+                sl_small.at[:, :, :, mine],
+                (b, to),
+            )
+        )
+    far_one = gather_forward(w1, near_one)
+    last_one = gather_last(w1, far_one)
+    finish(z_norms)
+    gains = [
+        jnp.concatenate([norms[q, r : r + 1, :] for q in range(4)], axis=1) for r in range(6)
+    ]
+    for copy in loads:
+        copy.wait()
+    finish(last_one)
+
+    def reduce_start(k, rows):
+        for r, row in enumerate(rows):
+            stat_a[k, b, r : r + 1, :] = jnp.sum(row, axis=0, keepdims=True)
+        for r in range(len(rows), 8):
+            stat_a[k, b, r : r + 1, :] = jnp.zeros((1, 512), F32)
+        return [send(stat_a.at[k, b], stat_a.at[k, b], peer) for peer in b_peers]
+
+    def reduce_middle(k, copies):
+        finish(copies)
+        stat_b[k, z] = jnp.sum(stat_a[k], axis=0)
+        return [send(stat_b.at[k, z], stat_b.at[k, z], peer) for peer in z_peers]
+
+    def reduce_end(k, copies):
+        finish(copies)
+        total = jnp.sum(stat_b[k], axis=0)
+        return [total[r : r + 1, :] for r in range(8)]
+
+    def chunk_big(i):
+        return pl.ds(pl.multiple_of(i * step_b, 16), step_b)
+
+    def chunk_small(i):
+        return pl.ds(pl.multiple_of(rows_b + i * step_s, 16), step_s)
+
+    def over_groups(body, count):
+        start = tuple(jnp.zeros((8, 512), F32) for _ in range(count))
+        big = lax.fori_loop(0, ob, lambda i, c: body(0, i, chunk_big(i), c), start)
+        small = lax.fori_loop(0, os_, lambda i, c: body(1, i, chunk_small(i), c), start)
+        return big, small
+
+    def moments(ref):
+        def body(group, i, rows, carry):
+            v = ref[rows, :]
+            return (carry[0] + fold(v), carry[1] + fold(v * v))
+
+        return over_groups(body, 2)
+
+    def both(big, small):
+        return jnp.concatenate([big.reshape(rows_b, -1), small.reshape(rows_s, -1)], axis=0)
+
+    def x_window(ta, tb):
+        half, odd = (lambda v: v // 2, lambda v: v % 2) if isinstance(ta, int) else (
+            lambda v: lax.div(v, 2), lambda v: lax.rem(v, 2)
+        )
+        hp, wp, sa, sb = odd(ta + 1), odd(tb + 1), half(ta), half(tb)
+        return both(
+            x_big[hp, wp, pl.ds(sa, ob), pl.ds(sb, ob)],
+            x_small[hp, wp, pl.ds(sa, os_), pl.ds(sb, os_)],
+        )
+
+    def dot(left, right):
+        return jnp.dot(left, right, preferred_element_type=F32)
+
+    def dot_t(left, right):
+        return lax.dot_general(left, right, (((1,), (1,)), ((), ())), preferred_element_type=F32)
+
+    def dot_rows(left, right):
+        return lax.dot_general(left, right, (((0,), (0,)), ((), ())), preferred_element_type=F32)
+
+    first_pre[...] = dot(x_window(0, 0), w1[0].reshape(256, 512))
+
+    def conv_one(t, _):
+        first_pre[...] += dot(x_window(lax.div(t, 3), lax.rem(t, 3)), w1[t].reshape(256, 512))
+        return 0
+
+    lax.fori_loop(1, 9, conv_one, 0)
+    proj_pre[...] = dot(x_window(1, 1), w1[9].reshape(256, 512))
+    first_big, first_small = moments(first_pre)
+    side_big, side_small = moments(proj_pre)
+    copies = reduce_start(0, first_big + first_small + side_big + side_small)
+    far_two = gather_forward(w2, near_two)
+    copies = reduce_middle(0, copies)
+    last_two = gather_last(w2, far_two)
+    sums = reduce_end(0, copies)
+
+    def centered(total, square, number):
+        center = total / number
+        return center, lax.rsqrt(square / number - center * center + NORM_EPS)
+
+    numbers = (number_big, number_small)
+    first_stat = [centered(sums[2 * g], sums[2 * g + 1], numbers[g]) for g in range(2)]
+    side_stat = [centered(sums[4 + 2 * g], sums[5 + 2 * g], numbers[g]) for g in range(2)]
+
+    def place(group, i, value, big, small, shift):
+        if group == 0:
+            big[i + shift, shift : shift + ob] = value.reshape(ob, nb_img, 512)
+        else:
+            small[i + shift, shift : shift + os_] = value.reshape(os_, ns_img, 512)
+
+    def hide(group, i, rows, carry):
+        center, factor = first_stat[group]
+        shaped = (first_pre[rows, :] - center) * factor * gains[0] + gains[1]
+        place(group, i, (shaped * jax.nn.sigmoid(shaped)).astype(BF16), h_big, h_small, 1)
+        return carry
+
+    over_groups(hide, 0)
+
+    finish(last_two)
+
+    def h_window(ta, tb):
+        return both(h_big[pl.ds(ta, ob), pl.ds(tb, ob)], h_small[pl.ds(ta, os_), pl.ds(tb, os_)])
+
+    second_pre[...] = dot(h_window(0, 0), w2[0].reshape(512, 512))
+
+    def conv_two(t, _):
+        second_pre[...] += dot(h_window(lax.div(t, 3), lax.rem(t, 3)), w2[t].reshape(512, 512))
+        return 0
+
+    lax.fori_loop(1, 9, conv_two, 0)
+    second_big, second_small = moments(second_pre)
+    copies = reduce_start(1, second_big + second_small)
+    finish(slope_copies)
+    copies = reduce_middle(1, copies)
+    sums = reduce_end(1, copies)
+    second_stat = [centered(sums[2 * g], sums[2 * g + 1], numbers[g]) for g in range(2)]
+
+    def normed(ref, stat, rows):
+        return (ref[rows, :] - stat[0]) * stat[1]
+
+    def outer(group, i, rows, carry):
+        two = normed(second_pre, second_stat[group], rows)
+        side = normed(proj_pre, side_stat[group], rows)
+        summed = two * gains[2] + gains[3] + side * gains[4] + gains[5]
+        gate = jax.nn.sigmoid(summed)
+        place(group, i, (summed * gate).astype(BF16), os_big, os_small, 0)
+        slope = sl_big[i] if group == 0 else sl_small[i]
+        slope = slope.astype(F32).reshape(two.shape)
+        upstream = slope * (gate * (1.0 + summed * (1.0 - gate)))
+        work[rows, :] = upstream
+        return (carry[0] + fold(upstream), carry[1] + fold(upstream * two), carry[2] + fold(upstream * side))
+
+    outer_big, outer_small = over_groups(outer, 3)
+    copies = reduce_start(2, outer_big + outer_small)
+    stores = []
+    for d in (1, 2, 3):
+        to = lax.rem(z + d, 4)
+        for staged, target, images in ((os_big, out_big, nb_img), (os_small, out_small, ns_img)):
+            send(
+                staged.at[:, :, :, lanes(to)],
+                target.at[:, :, pl.ds(pl.multiple_of(z * images, images), images)],
+                (b, to),
+            )
+            stores.append(started[-1])
+    for staged, target, images in ((os_big, out_big, nb_img), (os_small, out_small, ns_img)):
+        load(
+            staged.at[:, :, :, mine],
+            target.at[:, :, pl.ds(pl.multiple_of(z * images, images), images)],
+        )
+    copies = reduce_middle(2, copies)
+    sums_outer = reduce_end(2, copies)
+
+    def slopes(group, i, rows, carry):
+        total, cross_two, cross_side = sums_outer[3 * group : 3 * group + 3]
+        number = numbers[group]
+        two = normed(second_pre, second_stat[group], rows)
+        side = normed(proj_pre, side_stat[group], rows)
+        base = work[rows, :] - total / number
+        slope_two = gains[2] * second_stat[group][1] * (base - two * (cross_two / number))
+        slope_side = gains[4] * side_stat[group][1] * (base - side * (cross_side / number))
+        place(group, i, slope_two.astype(BF16), t_big, t_small, 1)
+        place(group, i, slope_side.astype(BF16), p_big, p_small, 0)
+        return carry
+
+    over_groups(slopes, 0)
+
+    def scatter_core(a, r, lo, n):
+        part = pl.ds(lo, n)
+        return send(a.at[part, :, :, 1 - core], r.at[part], sibling)
+
+    def scatter_near(a, r, rx, ry, lo, n, copy):
+        copy.wait_recv()
+        part = pl.ds(lo, n)
+
+        def add(t, _):
+            r[t] = (r[t].astype(F32) + a[t, :, :, core].astype(F32)).astype(BF16)
+            return 0
+
+        lax.fori_loop(lo, lo + n, add, 0)
+        return (
+            send(r.at[part, :, 1 - x, :, pl.ds(0, 256)], rx.at[part], x_peer),
+            send(r.at[part, 1 - y, :, :, pl.ds(256, 256)], ry.at[part], y_peer),
+        )
+
+    def scatter_far(r, rx, ry, rxx, ryy, lo, n, copies):
+        finish(copies)
+        part = pl.ds(lo, n)
+
+        def add(t, _):
+            rx[t] = (rx[t].astype(F32) + r[t, :, x, :, 0:256].astype(F32)).astype(BF16)
+            ry[t] = (ry[t].astype(F32) + r[t, y, :, :, 256:512].astype(F32)).astype(BF16)
+            return 0
+
+        lax.fori_loop(lo, lo + n, add, 0)
+        return (
+            send(rx.at[part, 1 - y], ryy.at[part], y_peer),
+            send(ry.at[part, 1 - x], rxx.at[part], x_peer),
+        )
+
+    def scatter_z(rx, ry, rxx, ryy, c, rz, lo, n, copies):
+        finish(copies)
+        part = pl.ds(lo, n)
+
+        def add(t, _):
+            c[t, :, 0:256] = (rx[t, y].astype(F32) + ryy[t].astype(F32)).astype(BF16)
+            c[t, :, 256:512] = (ry[t, x].astype(F32) + rxx[t].astype(F32)).astype(BF16)
+            return 0
+
+        lax.fori_loop(lo, lo + n, add, 0)
+        return [
+            send(c.at[part, :, lanes(lax.rem(z + d, 4))], rz.at[d - 1, part], (b, lax.rem(z + d, 4)))
+            for d in (1, 2, 3)
+        ]
+
+    def scatter_end(c, rz, out, lo, n, copies):
+        finish(copies)
+
+        def add(t, _):
+            total = c[t, :, mine].astype(F32)
+            for d in range(3):
+                total = total + rz[d, t].astype(F32)
+            out[t] = total
+            return 0
+
+        lax.fori_loop(lo, lo + n, add, 0)
+
+    t_flat = lambda: both(t_big[1 : ob + 1, 1 : ob + 1], t_small[1 : os_ + 1, 1 : os_ + 1])
+
+    def grad_two_taps(lo, n):
+        def tap(t, _):
+            d = dot_rows(h_window(lax.div(t, 3), lax.rem(t, 3)), t_flat())
+            a2[t] = d.astype(BF16).reshape(a2.shape[1:])
+            return 0
+
+        lax.fori_loop(lo, lo + n, tap, 0)
+
+    grad_two_taps(0, 3)
+    core_a = scatter_core(a2, r2, 0, 3)
+    grad_two_taps(3, 3)
+    core_b = scatter_core(a2, r2, 3, 3)
+    near_a = scatter_near(a2, r2, rx2, ry2, 0, 3, core_a)
+    grad_two_taps(6, 3)
+    core_c = scatter_core(a2, r2, 6, 3)
+    near_b = scatter_near(a2, r2, rx2, ry2, 3, 3, core_b)
+
+    def t_window(ta, tb):
+        return both(
+            t_big[pl.ds(2 - ta, ob), pl.ds(2 - tb, ob)],
+            t_small[pl.ds(2 - ta, os_), pl.ds(2 - tb, os_)],
+        )
+
+    work[...] = dot_t(t_window(0, 0), w2[0].reshape(512, 512))
+
+    def back_two(t, _):
+        work[...] += dot_t(t_window(lax.div(t, 3), lax.rem(t, 3)), w2[t].reshape(512, 512))
+        return 0
+
+    lax.fori_loop(1, 3, back_two, 0)
+    near_c = scatter_near(a2, r2, rx2, ry2, 6, 3, core_c)
+    lax.fori_loop(3, 9, back_two, 0)
+
+    def inner(group, i, rows, carry):
+        value = normed(first_pre, first_stat[group], rows)
+        e = work[rows, :] * silu_slope(value * gains[0] + gains[1])
+        work[rows, :] = e
+        return (carry[0] + fold(e), carry[1] + fold(e * value))
+
+    inner_big, inner_small = over_groups(inner, 2)
+    copies = reduce_start(3, inner_big + inner_small)
+    far_a = scatter_far(r2, rx2, ry2, rxx2, ryy2, 0, 3, near_a)
+    copies = reduce_middle(3, copies)
+    sums_inner = reduce_end(3, copies)
+
+    def slopes_one(group, i, rows, carry):
+        total, cross = sums_inner[2 * group : 2 * group + 2]
+        number = numbers[group]
+        value = normed(first_pre, first_stat[group], rows)
+        slope = gains[0] * first_stat[group][1] * (work[rows, :] - total / number - value * (cross / number))
+        place(group, i, slope.astype(BF16), s_big, s_small, 0)
+        return carry
+
+    over_groups(slopes_one, 0)
+
+    s_flat = lambda: both(s_big[0:ob, 0:ob], s_small[0:os_, 0:os_])
+    p_flat = lambda: both(p_big[...], p_small[...])
+
+    def grad_one_taps(lo, n):
+        def tap(t, _):
+            d = dot_rows(x_window(lax.div(t, 3), lax.rem(t, 3)), s_flat())
+            a1[t] = d.astype(BF16).reshape(a1.shape[1:])
+            return 0
+
+        lax.fori_loop(lo, lo + n, tap, 0)
+
+    grad_one_taps(0, 5)
+    core_d = scatter_core(a1, r1, 0, 5)
+    grad_one_taps(5, 4)
+    a1[9] = dot_rows(x_window(1, 1), p_flat()).astype(BF16).reshape(a1.shape[1:])
+    core_e = scatter_core(a1, r1, 5, 5)
+    near_d = scatter_near(a1, r1, rx1, ry1, 0, 5, core_d)
+    near_e = scatter_near(a1, r1, rx1, ry1, 5, 5, core_e)
+
+    def s_window(sa, sb):
+        return both(s_big[sa : sa + ob, sb : sb + ob], s_small[sa : sa + os_, sb : sb + os_])
+
+    def back_one(hp, wp):
+        total = dot_t(p_flat(), w1[9].reshape(256, 512)) if hp + wp == 0 else None
+        for ta in ((1,), (2, 0))[hp]:
+            for tb in ((1,), (2, 0))[wp]:
+                term = dot_t(
+                    s_window(int(ta == 0), int(tb == 0)), w1[3 * ta + tb].reshape(256, 512)
+                )
+                total = term if total is None else total + term
+        total = total.astype(BF16)
+        grad_big[:, hp, :, wp] = total[:rows_b].reshape(ob, ob, nb_img, 256)
+        grad_small[:, hp, :, wp] = total[rows_b:].reshape(os_, os_, ns_img, 256)
+
+    back_one(0, 0)
+    back_one(0, 1)
+    far_b = scatter_far(r2, rx2, ry2, rxx2, ryy2, 3, 3, near_b)
+    z_a = scatter_z(rx2, ry2, rxx2, ryy2, c2, rz2, 0, 3, far_a)
+    back_one(1, 0)
+    back_one(1, 1)
+
+    rows = [
+        sums_inner[1] + sums_inner[3],
+        sums_inner[0] + sums_inner[2],
+        sums_outer[1] + sums_outer[4],
+        sums_outer[0] + sums_outer[3],
+        sums_outer[2] + sums_outer[5],
+        sums_outer[0] + sums_outer[3],
+    ]
+    for r, row in enumerate(rows):
+        norm_rows[r : r + 1, :] = row
+    grad_norms[...] = norm_rows[0:6, mine]
+
+    far_c = scatter_far(r2, rx2, ry2, rxx2, ryy2, 6, 3, near_c)
+    z_b = scatter_z(rx2, ry2, rxx2, ryy2, c2, rz2, 3, 3, far_b)
+    far_d = scatter_far(r1, rx1, ry1, rxx1, ryy1, 0, 5, near_d)
+    z_c = scatter_z(rx2, ry2, rxx2, ryy2, c2, rz2, 6, 3, far_c)
+    far_e = scatter_far(r1, rx1, ry1, rxx1, ryy1, 5, 5, near_e)
+    z_d = scatter_z(rx1, ry1, rxx1, ryy1, c1, rz1, 0, 5, far_d)
+    scatter_end(c2, rz2, grad_two, 0, 3, z_a)
+    scatter_end(c2, rz2, grad_two, 3, 3, z_b)
+    z_e = scatter_z(rx1, ry1, rxx1, ryy1, c1, rz1, 5, 5, far_e)
+    scatter_end(c2, rz2, grad_two, 6, 3, z_c)
+    scatter_end(c1, rz1, grad_one, 0, 5, z_d)
+    scatter_end(c1, rz1, grad_one, 5, 5, z_e)
+    finish(stores)
+    for copy in loads[10:]:
+        copy.wait()
+    for copy in started:
+        copy.wait_send()
+    assert used[0] <= COPIES
 
 
 def tap_window(padded, tap_row, tap_col, stride, size_out):
@@ -100,21 +642,7 @@
     return gain * factor * (upstream - total / number - normed * (cross / number))
 
 
-def silu_slope(values):
-    gate = jax.nn.sigmoid(values)
-    return gate * (1.0 + values * (1.0 - gate))
-
-
-def adamw_step(weight, gradient, first, second, rate, decay):
-    first_new = BETA_ONE * first + (1.0 - BETA_ONE) * gradient
-    second_new = BETA_TWO * second + (1.0 - BETA_TWO) * gradient * gradient
-    first_hat = first_new / (1.0 - BETA_ONE**STEP)
-    second_hat = second_new / (1.0 - BETA_TWO**STEP)
-    updated = weight - rate * (first_hat / (jnp.sqrt(second_hat) + ADAM_EPS) + decay * weight)
-    return (updated, first_new, second_new)
-
-
-def body(
+def plain_body(
     image_big,
     image_small,
     slope_big,
@@ -368,50 +896,166 @@
     )
 
 
+def update_kernel(
+    g1, g2, gn,
+    w1, w2, wp, wn, f1, f2, fp, fn, s1, s2, sp, sn,
+    *outs,
+):
+    shape = w1.shape
+    grads = [
+        (g1[0:9].reshape(shape), w1, f1, s1, (9.0 * C_IN) ** (-0.5), DECAY),
+        (g2[...].reshape(w2.shape), w2, f2, s2, (9.0 * C_OUT) ** (-0.5), DECAY),
+        (g1[9], wp, fp, sp, (1.0 * C_IN) ** (-0.5), DECAY),
+        (gn[...], wn, fn, sn, NORM_RATE, 0.0),
+    ]
+    for i, (gradient, weight, first, second, rate, decay) in enumerate(grads):
+        new, moment, square = adamw_step(weight[...], gradient, first[...], second[...], rate, decay)
+        outs[i][...] = gradient
+        outs[4 + i][...] = new
+        outs[8 + i][...] = moment
+        outs[12 + i][...] = square
+
+
+def fused_body(
+    devices,
+    image_big, image_small, slope_big, slope_small,
+    conv1_weight, conv2_weight, proj_weight, norm_params,
+    first_conv1, first_conv2, first_proj, first_norms,
+    second_conv1, second_conv2, second_proj, second_norms,
+):
+    nb_img, side_b = image_big.shape[0], image_big.shape[1]
+    ns_img, side_s = image_small.shape[0], image_small.shape[1]
+    ob, os_ = side_b // 2, side_s // 2
+    rows = ob * ob * nb_img + os_ * os_ * ns_img
+    cfg = (nb_img, ns_img, ob, os_, ob * ob * nb_img * devices, os_ * os_ * ns_img * devices)
+    r1, r2 = conv1_weight.shape[2], conv2_weight.shape[2]
+
+    def parity(images, side):
+        images = jnp.transpose(images, (1, 2, 0, 3))
+        return images.reshape(side // 2, 2, side // 2, 2, images.shape[2], C_IN)
+
+    def flat(weight):
+        return weight.reshape((9,) + weight.shape[2:])
+
+    vmem = pl.BlockSpec(memory_space=pltpu.VMEM)
+    anywhere = pl.BlockSpec(memory_space=pl.ANY)
+    shape = jax.ShapeDtypeStruct
+    out_shape = (
+        shape((ob, ob, slope_big.shape[0], 128), BF16),
+        shape((os_, os_, slope_small.shape[0], 128), BF16),
+        shape((ob, 2, ob, 2, nb_img, C_IN), BF16),
+        shape((os_, 2, os_, 2, ns_img, C_IN), BF16),
+        shape((10, r1, 128), F32),
+        shape((9, r2, 128), F32),
+        shape((6, 128), F32),
+    )
+
+    def sum_buffers(taps, r):
+        return [
+            pltpu.VMEM((taps, 2, 2, 2, r, 512), BF16),
+            pltpu.VMEM((taps, 2, 2, r, 512), BF16),
+            pltpu.VMEM((taps, 2, r, 256), BF16),
+            pltpu.VMEM((taps, 2, r, 256), BF16),
+            pltpu.VMEM((taps, r, 256), BF16),
+            pltpu.VMEM((taps, r, 256), BF16),
+            pltpu.VMEM((taps, r, 512), BF16),
+            pltpu.VMEM((3, taps, r, 128), BF16),
+        ]
+
+    def maps(extra):
+        return [
+            pltpu.VMEM((ob + extra, ob + extra, nb_img, 512), BF16),
+            pltpu.VMEM((os_ + extra, os_ + extra, ns_img, 512), BF16),
+        ]
+
+    scratch = (
+        [
+            pltpu.VMEM((10, 2, 2, 2, r1, 512), BF16),
+            pltpu.VMEM((9, 2, 2, 2, r2, 512), BF16),
+            pltpu.VMEM((2, 2, ob + 1, ob + 1, nb_img, C_IN), BF16),
+            pltpu.VMEM((2, 2, os_ + 1, os_ + 1, ns_img, C_IN), BF16),
+        ]
+        + maps(2)
+        + [pltpu.VMEM((rows, 512), F32) for _ in range(4)]
+        + maps(0)
+        + maps(0)
+        + maps(2)
+        + maps(0)
+        + maps(1)
+        + [
+            pltpu.VMEM((4, 8, 128), F32),
+            pltpu.VMEM((8, 512), F32),
+            pltpu.VMEM((4, 8, 8, 512), F32),
+            pltpu.VMEM((4, 4, 8, 512), F32),
+        ]
+        + sum_buffers(10, r1)
+        + sum_buffers(9, r2)
+        + [
+            pltpu.SemaphoreType.DMA((COPIES,)),
+            pltpu.SemaphoreType.DMA((COPIES,)),
+            pltpu.SemaphoreType.DMA((12,)),
+        ]
+    )
+    macs = rows * 512 * (9 * C_IN + 9 * C_OUT + C_IN) * 3
+    out_big, out_small, grad_big, grad_small, grad_one, grad_two, grad_norms = pl.pallas_call(
+        functools.partial(block_kernel, cfg),
+        out_shape=out_shape,
+        in_specs=[anywhere] * 4 + [vmem] * 4,
+        out_specs=[anywhere] * 2 + [vmem] * 5,
+        scratch_shapes=scratch,
+        compiler_params=pltpu.CompilerParams(
+            collective_id=0, has_side_effects=True, vmem_limit_bytes=VMEM_BYTES
+        ),
+        cost_estimate=pl.CostEstimate(flops=2 * macs, bytes_accessed=1 << 23, transcendentals=rows * 2048),
+    )(
+        parity(image_big, side_b),
+        parity(image_small, side_s),
+        jnp.transpose(slope_big, (1, 2, 0, 3)),
+        jnp.transpose(slope_small, (1, 2, 0, 3)),
+        flat(conv1_weight),
+        flat(conv2_weight),
+        proj_weight,
+        norm_params,
+    )
+    weights = (conv1_weight, conv2_weight, proj_weight, norm_params)
+    updated = pl.pallas_call(
+        update_kernel,
+        out_shape=[shape(w.shape, F32) for w in weights] * 4,
+        in_specs=[vmem] * 15,
+        out_specs=[vmem] * 16,
+        compiler_params=pltpu.CompilerParams(vmem_limit_bytes=32 << 20),
+    )(
+        grad_one, grad_two, grad_norms,
+        *weights,
+        first_conv1, first_conv2, first_proj, first_norms,
+        second_conv1, second_conv2, second_proj, second_norms,
+    )
+
+    def unparity(images, side):
+        images = images.reshape(side, side, images.shape[4], C_IN)
+        return jnp.transpose(images, (2, 0, 1, 3))
+
+    return (
+        jnp.transpose(out_big, (2, 0, 1, 3)),
+        jnp.transpose(out_small, (2, 0, 1, 3)),
+        unparity(grad_big, side_b),
+        unparity(grad_small, side_s),
+        *updated,
+    )
+
+
 def solution(mesh):
-    placed = (
-        P(("batch", "chan"), None, None, None),
-        P(("batch", "chan"), None, None, None),
-        P("batch", None, None, "chan"),
-        P("batch", None, None, "chan"),
-        P(None, None, "batch", "chan"),
-        P(None, None, "batch", "chan"),
-        P("batch", "chan"),
-        P(None, "chan"),
-        P(None, None, "batch", "chan"),
-        P(None, None, "batch", "chan"),
-        P("batch", "chan"),
-        P(None, "chan"),
-        P(None, None, "batch", "chan"),
-        P(None, None, "batch", "chan"),
-        P("batch", "chan"),
-        P(None, "chan"),
-    )
+    images = P(("batch", "chan"), None, None, None)
+    maps = P("batch", None, None, "chan")
+    convs = P(None, None, "batch", "chan")
+    proj = P("batch", "chan")
+    norms = P(None, "chan")
+    states = (convs, convs, proj, norms)
+    fused = mesh.shape["batch"] == 8 and mesh.shape["chan"] == 4
     return jax.shard_map(
-        body,
+        functools.partial(fused_body, 32) if fused else plain_body,
         mesh=mesh,
-        in_specs=placed,
-        out_specs=(
-            P("batch", None, None, "chan"),
-            P("batch", None, None, "chan"),
-            P(("batch", "chan"), None, None, None),
-            P(("batch", "chan"), None, None, None),
-            P(None, None, "batch", "chan"),
-            P(None, None, "batch", "chan"),
-            P("batch", "chan"),
-            P(None, "chan"),
-            P(None, None, "batch", "chan"),
-            P(None, None, "batch", "chan"),
-            P("batch", "chan"),
-            P(None, "chan"),
-            P(None, None, "batch", "chan"),
-            P(None, None, "batch", "chan"),
-            P("batch", "chan"),
-            P(None, "chan"),
-            P(None, None, "batch", "chan"),
-            P(None, None, "batch", "chan"),
-            P("batch", "chan"),
-            P(None, "chan"),
-        ),
+        in_specs=(images, images, maps, maps) + states * 3,
+        out_specs=(maps, maps, images, images) + states * 4,
         check_vma=False,
     )

time: 1360 us -> 180 us (0.13); the launches traced: 1330 us -> 180 us
  waiting for transfers between devices: 546 us -> 0 us
  local copies, waits for them, and re-layouts: 367 us -> 7.67 us
  other arithmetic: 180 us -> 0 us
  Pallas kernels: 0 us -> 171 us
  matrix products: 148 us -> 0 us
  blocking collectives: 74.6 us -> 0 us
  between operations: 15.9 us -> 0.88 us
    reduce_scatter x6 -> x0, waiting for transfers between devices: 317 us -> none  [the longest x1 217 us: body(): lax.psum_scatter(input_part_big, 'chan', scatter_dimension=0, tiled=True)]
    all_gather x5 -> x0, waiting for transfers between devices: 228 us -> none  [the longest x1 113 us: body(): lax.all_gather(image_big, 'chan', axis=0, tiled=True)]
    pallas_call x0 -> x2, Pallas kernels: none -> 171 us  [the longest x1 170 us: fused_body(): pl.pallas_call(functools.partial(block_kernel, cfg), out_shape=out_shape,...]
    pad x8 -> x0, local copies, waits for them, and re-layouts: 147 us -> none  [the longest x6 112 us: input_grad(): lax.pad(term, jnp.float32(0.0), ((0, 0, 0), (tap_row, full_size - tap_row...]
    slice x8 -> x0, local copies, waits for them, and re-layouts: 140 us -> none  [input_grad(): return summed[:, 1:-1, 1:-1, :]]
    add x10 -> x0, other arithmetic: 132 us -> none  [the longest x6 73.5 us: input_grad(): summed + lax.pad(term, jnp.float32(0.0), ((0, 0, 0), (tap_row, full_size...]
    dot_general x106 -> x0, matrix products: 116 us -> none  [the longest x28 46.2 us: input_grad(): jnp.einsum('nhwo,co->nhwc', slope, kernel[tap_row, tap_col], preferred_el...]
    unnamed x203 -> x40, local copies, waits for them, and re-layouts: 78.8 us -> 7.67 us
  transfers between devices with their start and end apart: 12 -> 0, of which waited for: 7 -> 0; matrix products, arithmetic and copies ran while one was open for 48% -> 0% of each run, Pallas kernels for 0% -> 0%
where the time goes in v1:
time: 180 us
  Pallas kernels  171 us (95%)
  local copies, waits for them, and re-layouts  7.67 us (4%)
    pallas_call x1, Pallas kernels, fused_body(): pl.pallas_call(functools.partial(block_kernel, cfg), out_shape=out_shape,...  170 us
    unnamed x40, local copies, waits for them, and re-layouts  7.67 us

profile of v1, /device:TPU:0, one launch (start us, length us, event | category | flops | bytes accessed | tf_op | source)
XLA Modules:
  0.0 179.8 jit_solution(4767515414412930807)
XLA Ops:
  0.7 0.0 copy-start
  0.8 169.8 %shard_map.311 = (bf16[7,7,64,128]{3,2,1,0:T(8,128)(2,1)}, bf16[3,3,128,128]{3,2,1,0:T(8,128)(2,1)}, bf16[7,2,7,2,16,256]{5,4,3,2,1,0:T(8,128)(2,1)}, bf16[3,2,3...) custom-call(bf16[7,2,7,2,16,256]{5,4,3,2,1,0:T(8,128)(2,1)} %bitcast.24, ...), custom_call_target="tpu_custom_call" | custom-call | flops 23605542912 | bytes 8388608 | tf_op jit(solution)/shard_map/pallas_call | solution.py:1000
  170.6 0.0 copy-done
  170.6 0.0 copy-done.1
  170.6 0.0 copy-done.2
  170.6 0.0 copy-done.5
  170.6 0.0 copy-done.6
  170.6 0.0 copy-done.7
  170.6 0.0 copy-done.8
  170.6 0.0 copy-done.9
  170.6 0.0 copy-done.10
  170.7 0.0 copy-done.11
  170.7 0.0 copy-done.12
  170.7 0.0 copy-done.13
  170.7 0.0 copy-start.3
  170.7 1.0 copy-done.3
  171.6 0.9 copy-done.4
  172.6 0.7 copy-done.14
  173.2 1.5 shard_map.312
  174.8 2.1 %copy.40 = bf16[64,7,7,128]{3,0,2,1:T(8,128)(2,1)} copy(bf16[64,7,7,128]{3,0,2,1:T(8,128)(2,1)} %bitcast.21) | data formatting | bytes 1605632
  176.8 0.7 copy.41
  177.6 1.2 copy.42
  178.7 0.3 copy-done.16
  179.0 0.8 copy.43
  (18 shorter events, 0.0 us)
Async XLA Ops:
  0.7 169.9 %copy-start = (f32[3,3,64,128]{3,2,1,0:T(8,128)S(1)}, f32[3,3,64,128]{3,2,1,0:T(8,128)}, u32[]{:S(2)}) copy-start(f32[3,3,64,128]{3,2,1,0:T(8,128)} %w2.1) | copy-start | bytes 884740
  0.7 169.9 %copy-start.1 = (f32[3,3,64,128]{3,2,1,0:T(8,128)S(1)}, f32[3,3,64,128]{3,2,1,0:T(8,128)}, u32[]{:S(2)}) copy-start(f32[3,3,64,128]{3,2,1,0:T(8,128)} %f2.1) | copy-start | bytes 884740
  0.7 169.9 %copy-start.2 = (f32[3,3,64,128]{3,2,1,0:T(8,128)S(1)}, f32[3,3,64,128]{3,2,1,0:T(8,128)}, u32[]{:S(2)}) copy-start(f32[3,3,64,128]{3,2,1,0:T(8,128)} %s2_.1) | copy-start | bytes 884740
  0.7 169.9 %copy-start.5 = (f32[3,3,32,128]{3,2,1,0:T(8,128)S(1)}, f32[3,3,32,128]{3,2,1,0:T(8,128)}, u32[]{:S(2)}) copy-start(f32[3,3,32,128]{3,2,1,0:T(8,128)} %w1.1) | copy-start | bytes 442372
  0.7 169.9 %copy-start.6 = (f32[3,3,32,128]{3,2,1,0:T(8,128)S(1)}, f32[3,3,32,128]{3,2,1,0:T(8,128)}, u32[]{:S(2)}) copy-start(f32[3,3,32,128]{3,2,1,0:T(8,128)} %f1.1) | copy-start | bytes 442372
  0.7 169.9 %copy-start.7 = (f32[3,3,32,128]{3,2,1,0:T(8,128)S(1)}, f32[3,3,32,128]{3,2,1,0:T(8,128)}, u32[]{:S(2)}) copy-start(f32[3,3,32,128]{3,2,1,0:T(8,128)} %s1_.1) | copy-start | bytes 442372
  0.7 169.9 %copy-start.8 = (f32[32,128]{1,0:T(8,128)S(1)}, f32[32,128]{1,0:T(8,128)}, u32[]{:S(2)}) copy-start(f32[32,128]{1,0:T(8,128)} %wp.1) | copy-start | bytes 49156
  0.7 169.9 %copy-start.9 = (f32[32,128]{1,0:T(8,128)S(1)}, f32[32,128]{1,0:T(8,128)}, u32[]{:S(2)}) copy-start(f32[32,128]{1,0:T(8,128)} %fp.1) | copy-start | bytes 49156
  0.7 169.9 %copy-start.10 = (f32[32,128]{1,0:T(8,128)S(1)}, f32[32,128]{1,0:T(8,128)}, u32[]{:S(2)}) copy-start(f32[32,128]{1,0:T(8,128)} %sp.1) | copy-start | bytes 49156
  0.8 169.9 %copy-start.11 = (f32[6,128]{1,0:T(8,128)S(1)}, f32[6,128]{1,0:T(8,128)}, u32[]{:S(2)}) copy-start(f32[6,128]{1,0:T(8,128)} %wn.1) | copy-start | bytes 9220
  0.8 169.9 %copy-start.12 = (f32[6,128]{1,0:T(8,128)S(1)}, f32[6,128]{1,0:T(8,128)}, u32[]{:S(2)}) copy-start(f32[6,128]{1,0:T(8,128)} %fn.1) | copy-start | bytes 9220
  0.8 169.9 %copy-start.13 = (f32[6,128]{1,0:T(8,128)S(1)}, f32[6,128]{1,0:T(8,128)}, u32[]{:S(2)}) copy-start(f32[6,128]{1,0:T(8,128)} %sn.1) | copy-start | bytes 9220
  170.7 1.0 copy-start.3
  171.6 0.9 copy-start.4
  172.6 0.7 copy-start.14
  173.2 3.6 %copy-start.17 = (bf16[3,3,128,128]{3,2,1,0:T(8,128)(2,1)S(1)}, bf16[3,3,128,128]{3,2,1,0:T(8,128)(2,1)}, u32[]{:S(2)}) copy-start(bf16[3,3,128,128]{3,2,1,0:T(8,128)(2,1)} %get-tuple-element.44) | copy-start | bytes 884740
  173.2 4.3 %copy-start.15 = (bf16[7,2,7,2,16,256]{5,4,3,2,1,0:T(8,128)(2,1)S(1)}, bf16[7,2,7,2,16,256]{5,4,3,2,1,0:T(8,128)(2,1)}, u32[]{:S(2)}) copy-start(bf16[7,2,7,2,16,256]{5,4,3,2,1,0:T(8,128)(2,1)} %get-tuple-element.45) | copy-start | bytes 4816900
  177.6 1.5 copy-start.16

commit v2 on v1

--- a/solution.py
+++ b/solution.py
@@ -116,44 +116,47 @@
 
     pl.semaphore_wait(barrier, 10)
 
-    def gather_z(w):
-        piece = w.at[:, y, x, core, :, mine]
-        return [send(piece, piece, peer) for peer in z_peers]
-
-    def gather_xy(w):
-        piece = w.at[:, y, x, core]
-        return [
-            send(piece, piece, x_peer),
-            send(piece, piece, y_peer),
-            send(piece, piece, sibling),
-        ]
-
-    def gather_forward(w, near):
-        near[0].wait_recv()
-        piece = w.at[:, y, 1 - x, core]
-        part = w.at[:, y, 1 - x, core, :, pl.ds(0, 256)]
-        far_a = send(part, part, y_peer)
-        sib_x = send(piece, piece, sibling)
-        near[1].wait_recv()
-        piece = w.at[:, 1 - y, x, core]
-        part = w.at[:, 1 - y, x, core, :, pl.ds(256, 256)]
-        far_b = send(part, part, x_peer)
-        sib_y = send(piece, piece, sibling)
-        return [far_a, far_b, near[2], sib_x, sib_y]
-
-    def gather_last(w, far):
-        far[0].wait_recv()
-        far[1].wait_recv()
-        piece = w.at[:, 1 - y, 1 - x, core]
-        return far[2:] + [send(piece, piece, sibling)]
-
     def finish(copies):
         for copy in copies:
             copy.wait_recv()
 
-    z_one = gather_z(w1)
+    class Gather:
+        def __init__(self, w, lo, n):
+            self.w, self.taps = w, pl.ds(lo, n)
+            piece = w.at[self.taps, y, x, core, :, mine]
+            self.over_z = [send(piece, piece, peer) for peer in z_peers]
+
+        def near(self):
+            finish(self.over_z)
+            piece = self.w.at[self.taps, y, x, core]
+            self.x_copy = send(piece, piece, x_peer)
+            self.y_copy = send(piece, piece, y_peer)
+            self.rest = [send(piece, piece, sibling)]
+
+        def far(self):
+            self.x_copy.wait_recv()
+            part = self.w.at[self.taps, y, 1 - x, core, :, pl.ds(0, 256)]
+            self.far_a = send(part, part, y_peer)
+            self.y_copy.wait_recv()
+            part = self.w.at[self.taps, 1 - y, x, core, :, pl.ds(256, 256)]
+            self.far_b = send(part, part, x_peer)
+            piece = self.w.at[self.taps, y, 1 - x, core]
+            self.rest.append(send(piece, piece, sibling))
+            piece = self.w.at[self.taps, 1 - y, x, core]
+            self.rest.append(send(piece, piece, sibling))
+
+        def last(self):
+            finish([self.far_a, self.far_b])
+            piece = self.w.at[self.taps, 1 - y, 1 - x, core]
+            self.rest.append(send(piece, piece, sibling))
+
+        def done(self):
+            finish(self.rest)
+
+    one_a = Gather(w1, 0, 5)
     z_norms = [send(norms.at[z], norms.at[z], peer) for peer in z_peers]
-    z_two = gather_z(w2)
+    one_b = Gather(w1, 5, 5)
+    two_a, two_b, two_c = (Gather(w2, lo, 3) for lo in (0, 3, 6))
 
     zero = functools.partial(jnp.zeros, dtype=BF16)
     for wp in range(2):
@@ -173,53 +176,51 @@
         ref[side] = zero((side + 1, images, 512))
         ref[:, side] = zero((side + 1, images, 512))
 
-    finish(z_one)
-    near_one = gather_xy(w1)
-    finish(z_two)
-    near_two = gather_xy(w2)
     slope_copies = []
-    for d in (1, 2, 3):
-        to = lax.rem(z + d, 4)
-        slope_copies.append(
-            send(
-                slo_big.at[:, :, pl.ds(pl.multiple_of(to * nb_img, nb_img), nb_img)],
-                sl_big.at[:, :, :, mine],
-                (b, to),
+
+    def slopes_over_z(source, target, lo, n, images):
+        for d in (1, 2, 3):
+            to = lax.rem(z + d, 4)
+            rows = pl.ds(pl.multiple_of(to * images, images), images)
+            slope_copies.append(
+                send(source.at[pl.ds(lo, n), :, rows], target.at[pl.ds(lo, n), :, :, mine], (b, to))
             )
-        )
-        slope_copies.append(
-            send(
-                slo_small.at[:, :, pl.ds(pl.multiple_of(to * ns_img, ns_img), ns_img)],
-                sl_small.at[:, :, :, mine],
-                (b, to),
-            )
-        )
-    far_one = gather_forward(w1, near_one)
-    last_one = gather_last(w1, far_one)
+
+    big_parts = ((0, 4), (4, ob - 4))
+    one_a.near()
+    one_b.near()
+    one_a.far()
+    one_b.far()
+    two_a.near()
+    two_b.near()
+    slopes_over_z(slo_big, sl_big, *big_parts[0], nb_img)
+    one_a.last()
+    one_b.last()
     finish(z_norms)
     gains = [
         jnp.concatenate([norms[q, r : r + 1, :] for q in range(4)], axis=1) for r in range(6)
     ]
     for copy in loads:
         copy.wait()
-    finish(last_one)
+    one_a.done()
+    one_b.done()
 
     def reduce_start(k, rows):
         for r, row in enumerate(rows):
             stat_a[k, b, r : r + 1, :] = jnp.sum(row, axis=0, keepdims=True)
-        for r in range(len(rows), 8):
-            stat_a[k, b, r : r + 1, :] = jnp.zeros((1, 512), F32)
-        return [send(stat_a.at[k, b], stat_a.at[k, b], peer) for peer in b_peers]
-
-    def reduce_middle(k, copies):
+        part = stat_a.at[k, b, pl.ds(0, len(rows))]
+        return [send(part, part, peer) for peer in b_peers]
+
+    def reduce_middle(k, n, copies):
         finish(copies)
-        stat_b[k, z] = jnp.sum(stat_a[k], axis=0)
-        return [send(stat_b.at[k, z], stat_b.at[k, z], peer) for peer in z_peers]
-
-    def reduce_end(k, copies):
+        stat_b[k, z, 0:n] = jnp.sum(stat_a[k, :, 0:n], axis=0)
+        part = stat_b.at[k, z, pl.ds(0, n)]
+        return [send(part, part, peer) for peer in z_peers]
+
+    def reduce_end(k, n, copies):
         finish(copies)
-        total = jnp.sum(stat_b[k], axis=0)
-        return [total[r : r + 1, :] for r in range(8)]
+        total = jnp.sum(stat_b[k, :, 0:n], axis=0)
+        return [total[r : r + 1, :] for r in range(n)]
 
     def chunk_big(i):
         return pl.ds(pl.multiple_of(i * step_b, 16), step_b)
@@ -273,10 +274,13 @@
     first_big, first_small = moments(first_pre)
     side_big, side_small = moments(proj_pre)
     copies = reduce_start(0, first_big + first_small + side_big + side_small)
-    far_two = gather_forward(w2, near_two)
-    copies = reduce_middle(0, copies)
-    last_two = gather_last(w2, far_two)
-    sums = reduce_end(0, copies)
+    two_c.near()
+    two_a.far()
+    copies = reduce_middle(0, 8, copies)
+    slopes_over_z(slo_big, sl_big, *big_parts[1], nb_img)
+    slopes_over_z(slo_small, sl_small, 0, os_, ns_img)
+    two_b.far()
+    sums = reduce_end(0, 8, copies)
 
     def centered(total, square, number):
         center = total / number
@@ -300,7 +304,8 @@
 
     over_groups(hide, 0)
 
-    finish(last_two)
+    two_a.last()
+    two_a.done()
 
     def h_window(ta, tb):
         return both(h_big[pl.ds(ta, ob), pl.ds(tb, ob)], h_small[pl.ds(ta, os_), pl.ds(tb, os_)])
@@ -311,12 +316,19 @@
         second_pre[...] += dot(h_window(lax.div(t, 3), lax.rem(t, 3)), w2[t].reshape(512, 512))
         return 0
 
-    lax.fori_loop(1, 9, conv_two, 0)
+    lax.fori_loop(1, 3, conv_two, 0)
+    two_c.far()
+    two_b.last()
+    two_b.done()
+    lax.fori_loop(3, 6, conv_two, 0)
+    two_c.last()
+    two_c.done()
+    lax.fori_loop(6, 9, conv_two, 0)
     second_big, second_small = moments(second_pre)
     copies = reduce_start(1, second_big + second_small)
     finish(slope_copies)
-    copies = reduce_middle(1, copies)
-    sums = reduce_end(1, copies)
+    copies = reduce_middle(1, 4, copies)
+    sums = reduce_end(1, 4, copies)
     second_stat = [centered(sums[2 * g], sums[2 * g + 1], numbers[g]) for g in range(2)]
 
     def normed(ref, stat, rows):
@@ -337,22 +349,23 @@
     outer_big, outer_small = over_groups(outer, 3)
     copies = reduce_start(2, outer_big + outer_small)
     stores = []
-    for d in (1, 2, 3):
-        to = lax.rem(z + d, 4)
-        for staged, target, images in ((os_big, out_big, nb_img), (os_small, out_small, ns_img)):
-            send(
-                staged.at[:, :, :, lanes(to)],
-                target.at[:, :, pl.ds(pl.multiple_of(z * images, images), images)],
-                (b, to),
+
+    def outputs_over_z(staged, target, lo, n, images):
+        rows = pl.ds(pl.multiple_of(z * images, images), images)
+        for d in (1, 2, 3):
+            to = lax.rem(z + d, 4)
+            stores.append(
+                send(staged.at[pl.ds(lo, n), :, :, lanes(to)], target.at[pl.ds(lo, n), :, rows], (b, to))
             )
-            stores.append(started[-1])
+
+    copies = reduce_middle(2, 6, copies)
+    outputs_over_z(os_small, out_small, 0, os_, ns_img)
     for staged, target, images in ((os_big, out_big, nb_img), (os_small, out_small, ns_img)):
         load(
             staged.at[:, :, :, mine],
             target.at[:, :, pl.ds(pl.multiple_of(z * images, images), images)],
         )
-    copies = reduce_middle(2, copies)
-    sums_outer = reduce_end(2, copies)
+    sums_outer = reduce_end(2, 6, copies)
 
     def slopes(group, i, rows, carry):
         total, cross_two, cross_side = sums_outer[3 * group : 3 * group + 3]
@@ -438,29 +451,25 @@
 
         lax.fori_loop(lo, lo + n, tap, 0)
 
-    grad_two_taps(0, 3)
-    core_a = scatter_core(a2, r2, 0, 3)
-    grad_two_taps(3, 3)
-    core_b = scatter_core(a2, r2, 3, 3)
-    near_a = scatter_near(a2, r2, rx2, ry2, 0, 3, core_a)
-    grad_two_taps(6, 3)
-    core_c = scatter_core(a2, r2, 6, 3)
-    near_b = scatter_near(a2, r2, rx2, ry2, 3, 3, core_b)
-
     def t_window(ta, tb):
         return both(
             t_big[pl.ds(2 - ta, ob), pl.ds(2 - tb, ob)],
             t_small[pl.ds(2 - ta, os_), pl.ds(2 - tb, os_)],
         )
 
-    work[...] = dot_t(t_window(0, 0), w2[0].reshape(512, 512))
-
     def back_two(t, _):
         work[...] += dot_t(t_window(lax.div(t, 3), lax.rem(t, 3)), w2[t].reshape(512, 512))
         return 0
 
+    grad_two_taps(0, 3)
+    core_a = scatter_core(a2, r2, 0, 3)
+    outputs_over_z(os_big, out_big, *big_parts[0], nb_img)
+    grad_two_taps(3, 3)
+    core_b = scatter_core(a2, r2, 3, 3)
+    near_a = scatter_near(a2, r2, rx2, ry2, 0, 3, core_a)
+    work[...] = dot_t(t_window(0, 0), w2[0].reshape(512, 512))
     lax.fori_loop(1, 3, back_two, 0)
-    near_c = scatter_near(a2, r2, rx2, ry2, 6, 3, core_c)
+    near_b = scatter_near(a2, r2, rx2, ry2, 3, 3, core_b)
     lax.fori_loop(3, 9, back_two, 0)
 
     def inner(group, i, rows, carry):
@@ -472,8 +481,13 @@
     inner_big, inner_small = over_groups(inner, 2)
     copies = reduce_start(3, inner_big + inner_small)
     far_a = scatter_far(r2, rx2, ry2, rxx2, ryy2, 0, 3, near_a)
-    copies = reduce_middle(3, copies)
-    sums_inner = reduce_end(3, copies)
+    grad_two_taps(6, 3)
+    core_c = scatter_core(a2, r2, 6, 3)
+    copies = reduce_middle(3, 4, copies)
+    near_c = scatter_near(a2, r2, rx2, ry2, 6, 3, core_c)
+    far_b = scatter_far(r2, rx2, ry2, rxx2, ryy2, 3, 3, near_b)
+    z_a = scatter_z(rx2, ry2, rxx2, ryy2, c2, rz2, 0, 3, far_a)
+    sums_inner = reduce_end(3, 4, copies)
 
     def slopes_one(group, i, rows, carry):
         total, cross = sums_inner[2 * group : 2 * group + 2]
@@ -503,6 +517,8 @@
     core_e = scatter_core(a1, r1, 5, 5)
     near_d = scatter_near(a1, r1, rx1, ry1, 0, 5, core_d)
     near_e = scatter_near(a1, r1, rx1, ry1, 5, 5, core_e)
+    z_b = scatter_z(rx2, ry2, rxx2, ryy2, c2, rz2, 3, 3, far_b)
+    outputs_over_z(os_big, out_big, *big_parts[1], nb_img)
 
     def s_window(sa, sb):
         return both(s_big[sa : sa + ob, sb : sb + ob], s_small[sa : sa + os_, sb : sb + os_])
@@ -521,9 +537,10 @@
 
     back_one(0, 0)
     back_one(0, 1)
-    far_b = scatter_far(r2, rx2, ry2, rxx2, ryy2, 3, 3, near_b)
-    z_a = scatter_z(rx2, ry2, rxx2, ryy2, c2, rz2, 0, 3, far_a)
+    far_c = scatter_far(r2, rx2, ry2, rxx2, ryy2, 6, 3, near_c)
     back_one(1, 0)
+    far_d = scatter_far(r1, rx1, ry1, rxx1, ryy1, 0, 5, near_d)
+    z_c = scatter_z(rx2, ry2, rxx2, ryy2, c2, rz2, 6, 3, far_c)
     back_one(1, 1)
 
     rows = [
@@ -538,10 +555,6 @@
         norm_rows[r : r + 1, :] = row
     grad_norms[...] = norm_rows[0:6, mine]
 
-    far_c = scatter_far(r2, rx2, ry2, rxx2, ryy2, 6, 3, near_c)
-    z_b = scatter_z(rx2, ry2, rxx2, ryy2, c2, rz2, 3, 3, far_b)
-    far_d = scatter_far(r1, rx1, ry1, rxx1, ryy1, 0, 5, near_d)
-    z_c = scatter_z(rx2, ry2, rxx2, ryy2, c2, rz2, 6, 3, far_c)
     far_e = scatter_far(r1, rx1, ry1, rxx1, ryy1, 5, 5, near_e)
     z_d = scatter_z(rx1, ry1, rxx1, ryy1, c1, rz1, 0, 5, far_d)
     scatter_end(c2, rz2, grad_two, 0, 3, z_a)
@@ -896,24 +909,29 @@
     )
 
 
-def update_kernel(
-    g1, g2, gn,
-    w1, w2, wp, wn, f1, f2, fp, fn, s1, s2, sp, sn,
-    *outs,
-):
-    shape = w1.shape
-    grads = [
-        (g1[0:9].reshape(shape), w1, f1, s1, (9.0 * C_IN) ** (-0.5), DECAY),
-        (g2[...].reshape(w2.shape), w2, f2, s2, (9.0 * C_OUT) ** (-0.5), DECAY),
-        (g1[9], wp, fp, sp, (1.0 * C_IN) ** (-0.5), DECAY),
-        (gn[...], wn, fn, sn, NORM_RATE, 0.0),
-    ]
-    for i, (gradient, weight, first, second, rate, decay) in enumerate(grads):
-        new, moment, square = adamw_step(weight[...], gradient, first[...], second[...], rate, decay)
-        outs[i][...] = gradient
-        outs[4 + i][...] = new
-        outs[8 + i][...] = moment
-        outs[12 + i][...] = square
+def update_kernel(*refs):
+    passed, sums, states, rest = refs[:4], refs[4:7], refs[7:19], refs[19:]
+    passed_out, outs, (g1, g2, gn, sem) = rest[:4], rest[4:20], rest[20:]
+    copies = [
+        pltpu.make_async_copy(src, dst, sem.at[i])
+        for i, (src, dst) in enumerate(zip(sums + passed, (g1, g2, gn) + passed_out))
+    ]
+    for copy in copies:
+        copy.start()
+    for copy in copies[:3]:
+        copy.wait()
+    w1, w2 = states[0], states[1]
+    grads = (g1[0:9].reshape(w1.shape), g2[...].reshape(w2.shape), g1[9], gn[...])
+    rates = ((9.0 * C_IN) ** (-0.5), (9.0 * C_OUT) ** (-0.5), (1.0 * C_IN) ** (-0.5), NORM_RATE)
+    for i in range(4):
+        weight, first, second = (states[i + 4 * k][...] for k in range(3))
+        new, moment, square = adamw_step(
+            weight, grads[i], first, second, rates[i], DECAY if i < 3 else 0.0
+        )
+        for k, value in enumerate((grads[i], new, moment, square)):
+            outs[i + 4 * k][...] = value
+    for copy in copies[3:]:
+        copy.wait()
 
 
 def fused_body(
@@ -1018,15 +1036,17 @@
         norm_params,
     )
     weights = (conv1_weight, conv2_weight, proj_weight, norm_params)
-    updated = pl.pallas_call(
+    passed = (out_big, out_small, grad_big, grad_small)
+    sums = (grad_one, grad_two, grad_norms)
+    out_big, out_small, grad_big, grad_small, *updated = pl.pallas_call(
         update_kernel,
-        out_shape=[shape(w.shape, F32) for w in weights] * 4,
-        in_specs=[vmem] * 15,
-        out_specs=[vmem] * 16,
+        out_shape=[shape(v.shape, v.dtype) for v in passed] + [shape(w.shape, F32) for w in weights] * 4,
+        in_specs=[anywhere] * 7 + [vmem] * 12,
+        out_specs=[anywhere] * 4 + [vmem] * 16,
+        scratch_shapes=[pltpu.VMEM(v.shape, F32) for v in sums] + [pltpu.SemaphoreType.DMA((7,))],
         compiler_params=pltpu.CompilerParams(vmem_limit_bytes=32 << 20),
     )(
-        grad_one, grad_two, grad_norms,
-        *weights,
+        *passed, *sums, *weights,
         first_conv1, first_conv2, first_proj, first_norms,
         second_conv1, second_conv2, second_proj, second_norms,
     )

time: 180 us -> 144 us (0.80)
  Pallas kernels: 171 us -> 136 us
    pallas_call x1, Pallas kernels: 170 us -> 132 us  [fused_body(): pl.pallas_call(functools.partial(block_kernel, cfg), out_shape=out_shape,...]
    unnamed x40 -> x38, local copies, waits for them, and re-layouts: 7.67 us -> 7.18 us
where the time goes in v2:
time: 144 us
  Pallas kernels  136 us (94%)
  local copies, waits for them, and re-layouts  7.18 us (5%)
    pallas_call x1, Pallas kernels, fused_body(): pl.pallas_call(functools.partial(block_kernel, cfg), out_shape=out_shape,...  132 us
    unnamed x38, local copies, waits for them, and re-layouts  7.18 us
    pallas_call x1, Pallas kernels, fused_body(): pl.pallas_call(update_kernel, out_shape=[shape(v.shape, v.dtype) for v in...  3.25 us

profile of v2, /device:TPU:0, one launch (start us, length us, event | category | flops | bytes accessed | tf_op | source)
XLA Modules:
  0.0 143.7 jit_solution(12926765614193204603)
XLA Ops:
  0.7 0.0 copy-start.3
  0.7 0.0 copy-start.4
  0.7 0.0 copy-start.5
  0.7 0.0 copy-start.9
  0.7 0.0 copy-start.10
  0.7 0.0 copy-start.11
  0.7 0.0 copy-start.12
  0.7 0.0 copy-start.13
  0.7 0.0 copy-start.14
  0.8 0.0 copy-start.15
  0.8 0.0 copy-start.16
  0.8 0.0 copy-start.17
  0.8 132.4 %shard_map.311 = (bf16[7,7,64,128]{3,2,1,0:T(8,128)(2,1)}, bf16[3,3,128,128]{3,2,1,0:T(8,128)(2,1)}, bf16[7,2,7,2,16,256]{5,4,3,2,1,0:T(8,128)(2,1)}, bf16[3,2,3...) custom-call(bf16[7,2,7,2,16,256]{5,4,3,2,1,0:T(8,128)(2,1)} %bitcast.20, ...), custom_call_target="tpu_custom_call" | custom-call | flops 23605542912 | bytes 8388608 | tf_op jit(solution)/shard_map/pallas_call | solution.py:1018
  133.2 0.0 copy-done.3
  133.2 0.0 copy-done.4
  133.2 0.0 copy-done.5
  133.3 1.4 copy-done
  134.7 1.1 copy-done.1
  135.9 1.1 copy-done.2
  136.9 1.0 copy-done.6
  137.9 1.0 copy-done.7
  138.9 0.9 copy-done.8
  139.8 0.7 copy-done.18
  140.5 3.3 %shard_map.312 = (bf16[7,7,64,128]{3,2,1,0:T(8,128)(2,1)}, bf16[3,3,128,128]{3,2,1,0:T(8,128)(2,1)}, bf16[7,2,7,2,16,256]{5,4,3,2,1,0:T(8,128)(2,1)}, bf16[3,2,3...) custom-call(bf16[7,7,64,128]{3,2,1,0:T(8,128)(2,1)S(1)} %copy-done.1, ...), custom_call_target="tpu_custom_call" | custom-call | tf_op jit(solution)/shard_map/pallas_call | solution.py:1041
  (16 shorter events, 0.0 us)
Async XLA Ops:
  0.7 132.5 %copy-start.3 = (f32[3,3,64,128]{3,2,1,0:T(8,128)S(1)}, f32[3,3,64,128]{3,2,1,0:T(8,128)}, u32[]{:S(2)}) copy-start(f32[3,3,64,128]{3,2,1,0:T(8,128)} %refs_8_.1) | copy-start | bytes 884740
  0.7 132.5 %copy-start.4 = (f32[3,3,64,128]{3,2,1,0:T(8,128)S(1)}, f32[3,3,64,128]{3,2,1,0:T(8,128)}, u32[]{:S(2)}) copy-start(f32[3,3,64,128]{3,2,1,0:T(8,128)} %refs_12_.1) | copy-start | bytes 884740
  0.7 132.5 %copy-start.5 = (f32[3,3,64,128]{3,2,1,0:T(8,128)S(1)}, f32[3,3,64,128]{3,2,1,0:T(8,128)}, u32[]{:S(2)}) copy-start(f32[3,3,64,128]{3,2,1,0:T(8,128)} %refs_16_.1) | copy-start | bytes 884740
  0.7 132.5 %copy-start.9 = (f32[3,3,32,128]{3,2,1,0:T(8,128)S(1)}, f32[3,3,32,128]{3,2,1,0:T(8,128)}, u32[]{:S(2)}) copy-start(f32[3,3,32,128]{3,2,1,0:T(8,128)} %refs_7_.1) | copy-start | bytes 442372
  0.7 132.5 %copy-start.10 = (f32[3,3,32,128]{3,2,1,0:T(8,128)S(1)}, f32[3,3,32,128]{3,2,1,0:T(8,128)}, u32[]{:S(2)}) copy-start(f32[3,3,32,128]{3,2,1,0:T(8,128)} %refs_11_.1) | copy-start | bytes 442372
  0.7 132.5 %copy-start.11 = (f32[3,3,32,128]{3,2,1,0:T(8,128)S(1)}, f32[3,3,32,128]{3,2,1,0:T(8,128)}, u32[]{:S(2)}) copy-start(f32[3,3,32,128]{3,2,1,0:T(8,128)} %refs_15_.1) | copy-start | bytes 442372
  0.7 132.5 %copy-start.12 = (f32[32,128]{1,0:T(8,128)S(1)}, f32[32,128]{1,0:T(8,128)}, u32[]{:S(2)}) copy-start(f32[32,128]{1,0:T(8,128)} %refs_9_.1) | copy-start | bytes 49156
  0.7 132.5 %copy-start.13 = (f32[32,128]{1,0:T(8,128)S(1)}, f32[32,128]{1,0:T(8,128)}, u32[]{:S(2)}) copy-start(f32[32,128]{1,0:T(8,128)} %refs_13_.1) | copy-start | bytes 49156
  0.7 132.5 %copy-start.14 = (f32[32,128]{1,0:T(8,128)S(1)}, f32[32,128]{1,0:T(8,128)}, u32[]{:S(2)}) copy-start(f32[32,128]{1,0:T(8,128)} %refs_17_.1) | copy-start | bytes 49156
  0.8 132.5 %copy-start.15 = (f32[6,128]{1,0:T(8,128)S(1)}, f32[6,128]{1,0:T(8,128)}, u32[]{:S(2)}) copy-start(f32[6,128]{1,0:T(8,128)} %refs_10_.1) | copy-start | bytes 9220
  0.8 132.5 %copy-start.16 = (f32[6,128]{1,0:T(8,128)S(1)}, f32[6,128]{1,0:T(8,128)}, u32[]{:S(2)}) copy-start(f32[6,128]{1,0:T(8,128)} %refs_14_.1) | copy-start | bytes 9220
  0.8 132.5 %copy-start.17 = (f32[6,128]{1,0:T(8,128)S(1)}, f32[6,128]{1,0:T(8,128)}, u32[]{:S(2)}) copy-start(f32[6,128]{1,0:T(8,128)} %refs_18_.1) | copy-start | bytes 9220
  133.3 1.4 copy-start
  134.7 1.1 copy-start.1
  135.9 1.1 copy-start.2
  136.9 1.0 copy-start.6
  137.9 1.0 copy-start.7
  138.9 0.9 copy-start.8
  139.8 0.7 copy-start.18

commit v3 on v2

--- a/solution.py
+++ b/solution.py
@@ -19,8 +19,8 @@
 MESH = pl.DeviceIdType.MESH
 BF16 = jnp.bfloat16
 F32 = jnp.float32
-COPIES = 176
-VMEM_BYTES = 60 << 20
+COPIES = 192
+VMEM_BYTES = 58 << 20
 
 
 def silu_slope(values):
@@ -44,9 +44,9 @@
 
 def block_kernel(
     cfg,
-    img_big, img_small, slo_big, slo_small, w1_in, w2_in, wp_in, norms_in,
-    out_big, out_small, grad_big, grad_small, grad_one, grad_two, grad_norms,
-    w1, w2, x_big, x_small, h_big, h_small, first_pre, second_pre, proj_pre, work,
+    img_big, img_small, slo_big, slo_small, w1_hbm, w2_hbm, wp_hbm, norms_hbm,
+    out_big, out_small, grad_big, grad_small, grad_one_out, grad_two_out, grad_norms,
+    w1_in, w2_in, wp_in, norms_in, w1, w2, x_big, x_small, h_big, h_small, first_pre, second_pre, proj_pre, work, act,
     sl_big, sl_small, os_big, os_small, t_big, t_small, p_big, p_small, s_big, s_small,
     norms, norm_rows, stat_a, stat_b, a1, r1, rx1, ry1, rxx1, ryy1, c1, rz1,
     a2, r2, rx2, ry2, rxx2, ryy2, c2, rz2,
@@ -97,6 +97,8 @@
         copy.start()
         loads.append(copy)
 
+    for source, held in ((w1_hbm, w1_in), (w2_hbm, w2_in), (wp_hbm, wp_in), (norms_hbm, norms_in)):
+        load(source, held)
     for hp in range(2):
         for wp in range(2):
             load(img_big.at[:, hp, :, wp], x_big.at[hp, wp, pl.ds(hp, ob), pl.ds(wp, ob)])
@@ -109,6 +111,8 @@
         slo_small.at[:, :, pl.ds(pl.multiple_of(z * ns_img, ns_img), ns_img)],
         sl_small.at[:, :, :, mine],
     )
+    for copy in loads[:4]:
+        copy.wait()
     w1[0:9, y, x, core, :, mine] = w1_in[...].astype(BF16)
     w1[9, y, x, core, :, mine] = wp_in[...].astype(BF16)
     w2[:, y, x, core, :, mine] = w2_in[...].astype(BF16)
@@ -153,9 +157,9 @@
         def done(self):
             finish(self.rest)
 
-    one_a = Gather(w1, 0, 5)
+    one_a = Gather(w1, 0, 3)
     z_norms = [send(norms.at[z], norms.at[z], peer) for peer in z_peers]
-    one_b = Gather(w1, 5, 5)
+    one_b, one_c = Gather(w1, 3, 3), Gather(w1, 6, 4)
     two_a, two_b, two_c = (Gather(w2, lo, 3) for lo in (0, 3, 6))
 
     zero = functools.partial(jnp.zeros, dtype=BF16)
@@ -190,20 +194,25 @@
     one_a.near()
     one_b.near()
     one_a.far()
+    one_c.near()
     one_b.far()
     two_a.near()
+    one_c.far()
     two_b.near()
     slopes_over_z(slo_big, sl_big, *big_parts[0], nb_img)
     one_a.last()
     one_b.last()
+    one_c.last()
     finish(z_norms)
     gains = [
         jnp.concatenate([norms[q, r : r + 1, :] for q in range(4)], axis=1) for r in range(6)
     ]
-    for copy in loads:
+    for copy in loads[4:]:
         copy.wait()
+    two_c.near()
     one_a.done()
     one_b.done()
+    one_c.done()
 
     def reduce_start(k, rows):
         for r, row in enumerate(rows):
@@ -245,14 +254,24 @@
         return jnp.concatenate([big.reshape(rows_b, -1), small.reshape(rows_s, -1)], axis=0)
 
     def x_window(ta, tb):
-        half, odd = (lambda v: v // 2, lambda v: v % 2) if isinstance(ta, int) else (
-            lambda v: lax.div(v, 2), lambda v: lax.rem(v, 2)
+        hp, wp, sa, sb = (ta + 1) % 2, (tb + 1) % 2, ta // 2, tb // 2
+        return both(
+            x_big[hp, wp, sa : sa + ob, sb : sb + ob],
+            x_small[hp, wp, sa : sa + os_, sb : sb + os_],
         )
-        hp, wp, sa, sb = odd(ta + 1), odd(tb + 1), half(ta), half(tb)
-        return both(
-            x_big[hp, wp, pl.ds(sa, ob), pl.ds(sb, ob)],
-            x_small[hp, wp, pl.ds(sa, os_), pl.ds(sb, os_)],
-        )
+
+    def h_window(ta, tb):
+        return both(h_big[ta : ta + ob, tb : tb + ob], h_small[ta : ta + os_, tb : tb + os_])
+
+    def t_window(ta, tb):
+        ta, tb = 2 - ta, 2 - tb
+        return both(t_big[ta : ta + ob, tb : tb + ob], t_small[ta : ta + os_, tb : tb + os_])
+
+    def s_window(sa, sb):
+        return both(s_big[sa : sa + ob, sb : sb + ob], s_small[sa : sa + os_, sb : sb + os_])
+
+    def row_of(window, ta):
+        return jnp.concatenate([window(ta, tb) for tb in range(3)], axis=1)
 
     def dot(left, right):
         return jnp.dot(left, right, preferred_element_type=F32)
@@ -263,23 +282,27 @@
     def dot_rows(left, right):
         return lax.dot_general(left, right, (((0,), (0,)), ((), ())), preferred_element_type=F32)
 
-    first_pre[...] = dot(x_window(0, 0), w1[0].reshape(256, 512))
-
-    def conv_one(t, _):
-        first_pre[...] += dot(x_window(lax.div(t, 3), lax.rem(t, 3)), w1[t].reshape(256, 512))
-        return 0
-
-    lax.fori_loop(1, 9, conv_one, 0)
+    def conv_row(ref, window, w, depth, ta):
+        term = dot(row_of(window, ta), w[3 * ta : 3 * ta + 3].reshape(3 * depth, 512))
+        if ta == 0:
+            ref[...] = term
+        else:
+            ref[...] += term
+
+    for ta in range(3):
+        conv_row(first_pre, x_window, w1, 256, ta)
     proj_pre[...] = dot(x_window(1, 1), w1[9].reshape(256, 512))
     first_big, first_small = moments(first_pre)
     side_big, side_small = moments(proj_pre)
     copies = reduce_start(0, first_big + first_small + side_big + side_small)
-    two_c.near()
     two_a.far()
+    two_b.far()
     copies = reduce_middle(0, 8, copies)
     slopes_over_z(slo_big, sl_big, *big_parts[1], nb_img)
     slopes_over_z(slo_small, sl_small, 0, os_, ns_img)
-    two_b.far()
+    two_a.last()
+    two_c.far()
+    two_b.last()
     sums = reduce_end(0, 8, copies)
 
     def centered(total, square, number):
@@ -296,47 +319,43 @@
         else:
             small[i + shift, shift : shift + os_] = value.reshape(os_, ns_img, 512)
 
+    def normed(ref, stat, rows):
+        return (ref[rows, :] - stat[0]) * stat[1]
+
     def hide(group, i, rows, carry):
-        center, factor = first_stat[group]
-        shaped = (first_pre[rows, :] - center) * factor * gains[0] + gains[1]
+        value = normed(first_pre, first_stat[group], rows)
+        first_pre[rows, :] = value
+        shaped = value * gains[0] + gains[1]
         place(group, i, (shaped * jax.nn.sigmoid(shaped)).astype(BF16), h_big, h_small, 1)
         return carry
 
     over_groups(hide, 0)
 
-    two_a.last()
     two_a.done()
-
-    def h_window(ta, tb):
-        return both(h_big[pl.ds(ta, ob), pl.ds(tb, ob)], h_small[pl.ds(ta, os_), pl.ds(tb, os_)])
-
-    second_pre[...] = dot(h_window(0, 0), w2[0].reshape(512, 512))
-
-    def conv_two(t, _):
-        second_pre[...] += dot(h_window(lax.div(t, 3), lax.rem(t, 3)), w2[t].reshape(512, 512))
-        return 0
-
-    lax.fori_loop(1, 3, conv_two, 0)
-    two_c.far()
-    two_b.last()
+    conv_row(second_pre, h_window, w2, 512, 0)
+    two_c.last()
     two_b.done()
-    lax.fori_loop(3, 6, conv_two, 0)
-    two_c.last()
+    conv_row(second_pre, h_window, w2, 512, 1)
     two_c.done()
-    lax.fori_loop(6, 9, conv_two, 0)
+    conv_row(second_pre, h_window, w2, 512, 2)
     second_big, second_small = moments(second_pre)
     copies = reduce_start(1, second_big + second_small)
+
+    def prepare(group, i, rows, carry):
+        proj_pre[rows, :] = normed(proj_pre, side_stat[group], rows)
+        act[rows, :] = silu_slope(first_pre[rows, :] * gains[0] + gains[1])
+        return carry
+
+    over_groups(prepare, 0)
+    copies = reduce_middle(1, 4, copies)
     finish(slope_copies)
-    copies = reduce_middle(1, 4, copies)
     sums = reduce_end(1, 4, copies)
     second_stat = [centered(sums[2 * g], sums[2 * g + 1], numbers[g]) for g in range(2)]
 
-    def normed(ref, stat, rows):
-        return (ref[rows, :] - stat[0]) * stat[1]
-
     def outer(group, i, rows, carry):
         two = normed(second_pre, second_stat[group], rows)
-        side = normed(proj_pre, side_stat[group], rows)
+        second_pre[rows, :] = two
+        side = proj_pre[rows, :]
         summed = two * gains[2] + gains[3] + side * gains[4] + gains[5]
         gate = jax.nn.sigmoid(summed)
         place(group, i, (summed * gate).astype(BF16), os_big, os_small, 0)
@@ -370,158 +389,154 @@
     def slopes(group, i, rows, carry):
         total, cross_two, cross_side = sums_outer[3 * group : 3 * group + 3]
         number = numbers[group]
-        two = normed(second_pre, second_stat[group], rows)
-        side = normed(proj_pre, side_stat[group], rows)
         base = work[rows, :] - total / number
-        slope_two = gains[2] * second_stat[group][1] * (base - two * (cross_two / number))
-        slope_side = gains[4] * side_stat[group][1] * (base - side * (cross_side / number))
+        slope_two = gains[2] * second_stat[group][1] * (base - second_pre[rows, :] * (cross_two / number))
+        slope_side = gains[4] * side_stat[group][1] * (base - proj_pre[rows, :] * (cross_side / number))
         place(group, i, slope_two.astype(BF16), t_big, t_small, 1)
         place(group, i, slope_side.astype(BF16), p_big, p_small, 0)
         return carry
 
     over_groups(slopes, 0)
 
-    def scatter_core(a, r, lo, n):
-        part = pl.ds(lo, n)
-        return send(a.at[part, :, :, 1 - core], r.at[part], sibling)
-
-    def scatter_near(a, r, rx, ry, lo, n, copy):
-        copy.wait_recv()
-        part = pl.ds(lo, n)
-
-        def add(t, _):
-            r[t] = (r[t].astype(F32) + a[t, :, :, core].astype(F32)).astype(BF16)
-            return 0
-
-        lax.fori_loop(lo, lo + n, add, 0)
-        return (
-            send(r.at[part, :, 1 - x, :, pl.ds(0, 256)], rx.at[part], x_peer),
-            send(r.at[part, 1 - y, :, :, pl.ds(256, 256)], ry.at[part], y_peer),
-        )
-
-    def scatter_far(r, rx, ry, rxx, ryy, lo, n, copies):
-        finish(copies)
-        part = pl.ds(lo, n)
-
-        def add(t, _):
-            rx[t] = (rx[t].astype(F32) + r[t, :, x, :, 0:256].astype(F32)).astype(BF16)
-            ry[t] = (ry[t].astype(F32) + r[t, y, :, :, 256:512].astype(F32)).astype(BF16)
-            return 0
-
-        lax.fori_loop(lo, lo + n, add, 0)
-        return (
-            send(rx.at[part, 1 - y], ryy.at[part], y_peer),
-            send(ry.at[part, 1 - x], rxx.at[part], x_peer),
-        )
-
-    def scatter_z(rx, ry, rxx, ryy, c, rz, lo, n, copies):
-        finish(copies)
-        part = pl.ds(lo, n)
-
-        def add(t, _):
-            c[t, :, 0:256] = (rx[t, y].astype(F32) + ryy[t].astype(F32)).astype(BF16)
-            c[t, :, 256:512] = (ry[t, x].astype(F32) + rxx[t].astype(F32)).astype(BF16)
-            return 0
-
-        lax.fori_loop(lo, lo + n, add, 0)
-        return [
-            send(c.at[part, :, lanes(lax.rem(z + d, 4))], rz.at[d - 1, part], (b, lax.rem(z + d, 4)))
-            for d in (1, 2, 3)
-        ]
-
-    def scatter_end(c, rz, out, lo, n, copies):
-        finish(copies)
-
-        def add(t, _):
-            total = c[t, :, mine].astype(F32)
-            for d in range(3):
-                total = total + rz[d, t].astype(F32)
-            out[t] = total
-            return 0
-
-        lax.fori_loop(lo, lo + n, add, 0)
+    class Scatter:
+        def __init__(self, bufs, lo, n):
+            self.bufs, self.taps = bufs, pl.ds(lo, n)
+            self.loop = lambda body: lax.fori_loop(lo, lo + n, lambda t, c: (body(t), c)[1], 0)
+            a, r = bufs[0], bufs[1]
+            self.copies = [send(a.at[self.taps, :, :, 1 - core], r.at[self.taps], sibling)]
+
+        def near(self):
+            finish(self.copies)
+            a, r, rx, ry = self.bufs[:4]
+
+            def add(t):
+                r[t] = (r[t].astype(F32) + a[t, :, :, core].astype(F32)).astype(BF16)
+
+            self.loop(add)
+            taps = self.taps
+            self.copies = [
+                send(r.at[taps, :, 1 - x, :, pl.ds(0, 256)], rx.at[taps], x_peer),
+                send(r.at[taps, 1 - y, :, :, pl.ds(256, 256)], ry.at[taps], y_peer),
+            ]
+
+        def far(self):
+            finish(self.copies)
+            _, r, rx, ry, rxx, ryy = self.bufs[:6]
+
+            def add(t):
+                rx[t] = (rx[t].astype(F32) + r[t, :, x, :, 0:256].astype(F32)).astype(BF16)
+                ry[t] = (ry[t].astype(F32) + r[t, y, :, :, 256:512].astype(F32)).astype(BF16)
+
+            self.loop(add)
+            taps = self.taps
+            self.copies = [
+                send(rx.at[taps, 1 - y], ryy.at[taps], y_peer),
+                send(ry.at[taps, 1 - x], rxx.at[taps], x_peer),
+            ]
+
+        def over_z(self):
+            finish(self.copies)
+            rx, ry, rxx, ryy, c, rz = self.bufs[2:8]
+
+            def add(t):
+                c[t, :, 0:256] = (rx[t, y].astype(F32) + ryy[t].astype(F32)).astype(BF16)
+                c[t, :, 256:512] = (ry[t, x].astype(F32) + rxx[t].astype(F32)).astype(BF16)
+
+            self.loop(add)
+            self.copies = [
+                send(
+                    c.at[self.taps, :, lanes(lax.rem(z + d, 4))],
+                    rz.at[d - 1, self.taps],
+                    (b, lax.rem(z + d, 4)),
+                )
+                for d in (1, 2, 3)
+            ]
+
+        def end(self):
+            finish(self.copies)
+            c, rz, out = self.bufs[6:]
+
+            def add(t):
+                total = c[t, :, mine].astype(F32)
+                for d in range(3):
+                    total = total + rz[d, t].astype(F32)
+                out[t] = total
+
+            self.loop(add)
 
     t_flat = lambda: both(t_big[1 : ob + 1, 1 : ob + 1], t_small[1 : os_ + 1, 1 : os_ + 1])
-
-    def grad_two_taps(lo, n):
-        def tap(t, _):
-            d = dot_rows(h_window(lax.div(t, 3), lax.rem(t, 3)), t_flat())
-            a2[t] = d.astype(BF16).reshape(a2.shape[1:])
-            return 0
-
-        lax.fori_loop(lo, lo + n, tap, 0)
-
-    def t_window(ta, tb):
-        return both(
-            t_big[pl.ds(2 - ta, ob), pl.ds(2 - tb, ob)],
-            t_small[pl.ds(2 - ta, os_), pl.ds(2 - tb, os_)],
-        )
-
-    def back_two(t, _):
-        work[...] += dot_t(t_window(lax.div(t, 3), lax.rem(t, 3)), w2[t].reshape(512, 512))
-        return 0
-
-    grad_two_taps(0, 3)
-    core_a = scatter_core(a2, r2, 0, 3)
+    s_flat = lambda: both(s_big[0:ob, 0:ob], s_small[0:os_, 0:os_])
+    p_flat = lambda: both(p_big[...], p_small[...])
+
+    def grad_two(lo, n):
+        for t in range(lo, lo + n):
+            a2[t] = dot_rows(h_window(t // 3, t % 3), t_flat()).astype(BF16).reshape(a2.shape[1:])
+        return Scatter((a2, r2, rx2, ry2, rxx2, ryy2, c2, rz2, grad_two_out), lo, n)
+
+    def grad_one(ta, proj):
+        sums = dot_rows(row_of(x_window, ta), s_flat()).astype(BF16)
+        a1[3 * ta : 3 * ta + 3] = sums.reshape((3,) + a1.shape[1:])
+        if proj:
+            a1[9] = dot_rows(x_window(1, 1), p_flat()).astype(BF16).reshape(a1.shape[1:])
+        return Scatter((a1, r1, rx1, ry1, rxx1, ryy1, c1, rz1, grad_one_out), 3 * ta, 4 if proj else 3)
+
+    def back_row(ta):
+        term = None
+        for tb in range(3):
+            part = dot_t(t_window(ta, tb), w2[3 * ta + tb].reshape(512, 512))
+            term = part if term is None else term + part
+        if ta == 0:
+            work[...] = term
+        else:
+            work[...] += term
+
+    sum_a = grad_two(0, 2)
+    sum_b = grad_two(2, 2)
+    sum_a.near()
+    back_row(0)
+    sum_b.near()
     outputs_over_z(os_big, out_big, *big_parts[0], nb_img)
-    grad_two_taps(3, 3)
-    core_b = scatter_core(a2, r2, 3, 3)
-    near_a = scatter_near(a2, r2, rx2, ry2, 0, 3, core_a)
-    work[...] = dot_t(t_window(0, 0), w2[0].reshape(512, 512))
-    lax.fori_loop(1, 3, back_two, 0)
-    near_b = scatter_near(a2, r2, rx2, ry2, 3, 3, core_b)
-    lax.fori_loop(3, 9, back_two, 0)
+    back_row(1)
+    back_row(2)
 
     def inner(group, i, rows, carry):
-        value = normed(first_pre, first_stat[group], rows)
-        e = work[rows, :] * silu_slope(value * gains[0] + gains[1])
+        e = work[rows, :] * act[rows, :]
         work[rows, :] = e
-        return (carry[0] + fold(e), carry[1] + fold(e * value))
+        return (carry[0] + fold(e), carry[1] + fold(e * first_pre[rows, :]))
 
     inner_big, inner_small = over_groups(inner, 2)
     copies = reduce_start(3, inner_big + inner_small)
-    far_a = scatter_far(r2, rx2, ry2, rxx2, ryy2, 0, 3, near_a)
-    grad_two_taps(6, 3)
-    core_c = scatter_core(a2, r2, 6, 3)
+    sum_a.far()
+    sum_c = grad_two(4, 2)
+    sum_b.far()
+    sum_d = grad_two(6, 3)
+    sum_c.near()
     copies = reduce_middle(3, 4, copies)
-    near_c = scatter_near(a2, r2, rx2, ry2, 6, 3, core_c)
-    far_b = scatter_far(r2, rx2, ry2, rxx2, ryy2, 3, 3, near_b)
-    z_a = scatter_z(rx2, ry2, rxx2, ryy2, c2, rz2, 0, 3, far_a)
+    sum_d.near()
+    sum_a.over_z()
+    sum_b.over_z()
     sums_inner = reduce_end(3, 4, copies)
 
     def slopes_one(group, i, rows, carry):
         total, cross = sums_inner[2 * group : 2 * group + 2]
         number = numbers[group]
-        value = normed(first_pre, first_stat[group], rows)
-        slope = gains[0] * first_stat[group][1] * (work[rows, :] - total / number - value * (cross / number))
+        slope = gains[0] * first_stat[group][1] * (
+            work[rows, :] - total / number - first_pre[rows, :] * (cross / number)
+        )
         place(group, i, slope.astype(BF16), s_big, s_small, 0)
         return carry
 
     over_groups(slopes_one, 0)
 
-    s_flat = lambda: both(s_big[0:ob, 0:ob], s_small[0:os_, 0:os_])
-    p_flat = lambda: both(p_big[...], p_small[...])
-
-    def grad_one_taps(lo, n):
-        def tap(t, _):
-            d = dot_rows(x_window(lax.div(t, 3), lax.rem(t, 3)), s_flat())
-            a1[t] = d.astype(BF16).reshape(a1.shape[1:])
-            return 0
-
-        lax.fori_loop(lo, lo + n, tap, 0)
-
-    grad_one_taps(0, 5)
-    core_d = scatter_core(a1, r1, 0, 5)
-    grad_one_taps(5, 4)
-    a1[9] = dot_rows(x_window(1, 1), p_flat()).astype(BF16).reshape(a1.shape[1:])
-    core_e = scatter_core(a1, r1, 5, 5)
-    near_d = scatter_near(a1, r1, rx1, ry1, 0, 5, core_d)
-    near_e = scatter_near(a1, r1, rx1, ry1, 5, 5, core_e)
-    z_b = scatter_z(rx2, ry2, rxx2, ryy2, c2, rz2, 3, 3, far_b)
+    sum_e = grad_one(0, False)
     outputs_over_z(os_big, out_big, *big_parts[1], nb_img)
-
-    def s_window(sa, sb):
-        return both(s_big[sa : sa + ob, sb : sb + ob], s_small[sa : sa + os_, sb : sb + os_])
+    sum_c.far()
+    sum_f = grad_one(1, False)
+    sum_e.near()
+    sum_g = grad_one(2, True)
+    sum_f.near()
+    sum_d.far()
+    sum_g.near()
 
     def back_one(hp, wp):
         total = dot_t(p_flat(), w1[9].reshape(256, 512)) if hp + wp == 0 else None
@@ -537,12 +552,12 @@
 
     back_one(0, 0)
     back_one(0, 1)
-    far_c = scatter_far(r2, rx2, ry2, rxx2, ryy2, 6, 3, near_c)
+    sum_e.far()
     back_one(1, 0)
-    far_d = scatter_far(r1, rx1, ry1, rxx1, ryy1, 0, 5, near_d)
-    z_c = scatter_z(rx2, ry2, rxx2, ryy2, c2, rz2, 6, 3, far_c)
+    sum_f.far()
+    sum_c.over_z()
+    sum_g.far()
     back_one(1, 1)
-
     rows = [
         sums_inner[1] + sums_inner[3],
         sums_inner[0] + sums_inner[2],
@@ -554,17 +569,19 @@
     for r, row in enumerate(rows):
         norm_rows[r : r + 1, :] = row
     grad_norms[...] = norm_rows[0:6, mine]
-
-    far_e = scatter_far(r1, rx1, ry1, rxx1, ryy1, 5, 5, near_e)
-    z_d = scatter_z(rx1, ry1, rxx1, ryy1, c1, rz1, 0, 5, far_d)
-    scatter_end(c2, rz2, grad_two, 0, 3, z_a)
-    scatter_end(c2, rz2, grad_two, 3, 3, z_b)
-    z_e = scatter_z(rx1, ry1, rxx1, ryy1, c1, rz1, 5, 5, far_e)
-    scatter_end(c2, rz2, grad_two, 6, 3, z_c)
-    scatter_end(c1, rz1, grad_one, 0, 5, z_d)
-    scatter_end(c1, rz1, grad_one, 5, 5, z_e)
+    sum_d.over_z()
+    sum_e.over_z()
+    sum_f.over_z()
+    sum_a.end()
+    sum_b.end()
+    sum_g.over_z()
+    sum_c.end()
+    sum_d.end()
+    sum_e.end()
+    sum_f.end()
+    sum_g.end()
     finish(stores)
-    for copy in loads[10:]:
+    for copy in loads[14:]:
         copy.wait()
     for copy in started:
         copy.wait_send()
@@ -911,15 +928,14 @@
 
 def update_kernel(*refs):
     passed, sums, states, rest = refs[:4], refs[4:7], refs[7:19], refs[19:]
-    passed_out, outs, (g1, g2, gn, sem) = rest[:4], rest[4:20], rest[20:]
+    passed_out, outs, (sem,) = rest[:4], rest[4:20], rest[20:]
+    g1, g2, gn = sums
     copies = [
         pltpu.make_async_copy(src, dst, sem.at[i])
-        for i, (src, dst) in enumerate(zip(sums + passed, (g1, g2, gn) + passed_out))
+        for i, (src, dst) in enumerate(zip(passed, passed_out))
     ]
     for copy in copies:
         copy.start()
-    for copy in copies[:3]:
-        copy.wait()
     w1, w2 = states[0], states[1]
     grads = (g1[0:9].reshape(w1.shape), g2[...].reshape(w2.shape), g1[9], gn[...])
     rates = ((9.0 * C_IN) ** (-0.5), (9.0 * C_OUT) ** (-0.5), (1.0 * C_IN) ** (-0.5), NORM_RATE)
@@ -930,7 +946,7 @@
         )
         for k, value in enumerate((grads[i], new, moment, square)):
             outs[i + 4 * k][...] = value
-    for copy in copies[3:]:
+    for copy in copies:
         copy.wait()
 
 
@@ -957,15 +973,16 @@
 
     vmem = pl.BlockSpec(memory_space=pltpu.VMEM)
     anywhere = pl.BlockSpec(memory_space=pl.ANY)
+    hbm = pl.BlockSpec(memory_space=pltpu.HBM)
     shape = jax.ShapeDtypeStruct
     out_shape = (
-        shape((ob, ob, slope_big.shape[0], 128), BF16),
-        shape((os_, os_, slope_small.shape[0], 128), BF16),
-        shape((ob, 2, ob, 2, nb_img, C_IN), BF16),
-        shape((os_, 2, os_, 2, ns_img, C_IN), BF16),
-        shape((10, r1, 128), F32),
-        shape((9, r2, 128), F32),
-        shape((6, 128), F32),
+        pltpu.VMEM((ob, ob, slope_big.shape[0], 128), BF16),
+        pltpu.VMEM((os_, os_, slope_small.shape[0], 128), BF16),
+        pltpu.VMEM((ob, 2, ob, 2, nb_img, C_IN), BF16),
+        pltpu.VMEM((os_, 2, os_, 2, ns_img, C_IN), BF16),
+        pltpu.VMEM((10, r1, 128), F32),
+        pltpu.VMEM((9, r2, 128), F32),
+        pltpu.VMEM((6, 128), F32),
     )
 
     def sum_buffers(taps, r):
@@ -988,13 +1005,17 @@
 
     scratch = (
         [
+            pltpu.VMEM((9, r1, 128), F32),
+            pltpu.VMEM((9, r2, 128), F32),
+            pltpu.VMEM((r1, 128), F32),
+            pltpu.VMEM((6, 128), F32),
             pltpu.VMEM((10, 2, 2, 2, r1, 512), BF16),
             pltpu.VMEM((9, 2, 2, 2, r2, 512), BF16),
             pltpu.VMEM((2, 2, ob + 1, ob + 1, nb_img, C_IN), BF16),
             pltpu.VMEM((2, 2, os_ + 1, os_ + 1, ns_img, C_IN), BF16),
         ]
         + maps(2)
-        + [pltpu.VMEM((rows, 512), F32) for _ in range(4)]
+        + [pltpu.VMEM((rows, 512), F32) for _ in range(5)]
         + maps(0)
         + maps(0)
         + maps(2)
@@ -1011,14 +1032,14 @@
         + [
             pltpu.SemaphoreType.DMA((COPIES,)),
             pltpu.SemaphoreType.DMA((COPIES,)),
-            pltpu.SemaphoreType.DMA((12,)),
+            pltpu.SemaphoreType.DMA((16,)),
         ]
     )
     macs = rows * 512 * (9 * C_IN + 9 * C_OUT + C_IN) * 3
     out_big, out_small, grad_big, grad_small, grad_one, grad_two, grad_norms = pl.pallas_call(
         functools.partial(block_kernel, cfg),
         out_shape=out_shape,
-        in_specs=[anywhere] * 4 + [vmem] * 4,
+        in_specs=[hbm] * 8,
         out_specs=[anywhere] * 2 + [vmem] * 5,
         scratch_shapes=scratch,
         compiler_params=pltpu.CompilerParams(
@@ -1041,10 +1062,10 @@
     out_big, out_small, grad_big, grad_small, *updated = pl.pallas_call(
         update_kernel,
         out_shape=[shape(v.shape, v.dtype) for v in passed] + [shape(w.shape, F32) for w in weights] * 4,
-        in_specs=[anywhere] * 7 + [vmem] * 12,
+        in_specs=[vmem] * 19,
         out_specs=[anywhere] * 4 + [vmem] * 16,
-        scratch_shapes=[pltpu.VMEM(v.shape, F32) for v in sums] + [pltpu.SemaphoreType.DMA((7,))],
-        compiler_params=pltpu.CompilerParams(vmem_limit_bytes=32 << 20),
+        scratch_shapes=[pltpu.SemaphoreType.DMA((4,))],
+        compiler_params=pltpu.CompilerParams(vmem_limit_bytes=16 << 20),
     )(
         *passed, *sums, *weights,
         first_conv1, first_conv2, first_proj, first_norms,

time: 144 us -> 125 us (0.87)
  Pallas kernels: 136 us -> 124 us
  local copies, waits for them, and re-layouts: 7.18 us -> 0.05 us
    pallas_call x1, Pallas kernels: 132 us -> 121 us  [fused_body(): pl.pallas_call(functools.partial(block_kernel, cfg), out_shape=out_shape,...]
    unnamed x38 -> x24, local copies, waits for them, and re-layouts: 7.18 us -> 0.05 us
where the time goes in v3:
time: 125 us
  Pallas kernels  124 us (99%)
    pallas_call x1, Pallas kernels, fused_body(): pl.pallas_call(functools.partial(block_kernel, cfg), out_shape=out_shape,...  121 us
    pallas_call x1, Pallas kernels, fused_body(): pl.pallas_call(update_kernel, out_shape=[shape(v.shape, v.dtype) for v in...  3.03 us

profile of v3, /device:TPU:0, one launch (start us, length us, event | category | flops | bytes accessed | tf_op | source)
XLA Modules:
  0.0 125.3 jit_solution(12335453629301447524)
XLA Ops:
  0.7 0.0 copy-start
  0.7 0.0 copy-start.1
  0.7 0.0 copy-start.2
  0.7 0.0 copy-start.3
  0.7 0.0 copy-start.4
  0.7 0.0 copy-start.5
  0.7 0.0 copy-start.6
  0.7 0.0 copy-start.7
  0.7 0.0 copy-start.8
  0.8 0.0 copy-start.9
  0.8 0.0 copy-start.10
  0.8 0.0 copy-start.11
  0.8 121.2 %shard_map.311 = (bf16[7,7,64,128]{3,2,1,0:T(8,128)(2,1)S(1)}, bf16[3,3,128,128]{3,2,1,0:T(8,128)(2,1)S(1)}, bf16[7,2,7,2,16,256]{5,4,3,2,1,0:T(8,128)(2,1)S(1)}...) custom-call(bf16[7,2,7,2,16,256]{5,4,3,2,1,0:T(8,128)(2,1)} %bitcast, ...), custom_call_target="tpu_custom_call" | custom-call | flops 23605542912 | bytes 8388608 | tf_op jit(solution)/shard_map/pallas_call | solution.py:1039
  122.0 0.0 copy-done
  122.0 0.0 copy-done.1
  122.0 0.0 copy-done.2
  122.0 0.0 copy-done.3
  122.0 0.0 copy-done.4
  122.1 0.0 copy-done.5
  122.1 0.0 copy-done.6
  122.1 0.0 copy-done.7
  122.1 0.0 copy-done.8
  122.1 0.0 copy-done.9
  122.1 3.0 %shard_map.312 = (bf16[7,7,64,128]{3,2,1,0:T(8,128)(2,1)}, bf16[3,3,128,128]{3,2,1,0:T(8,128)(2,1)}, bf16[7,2,7,2,16,256]{5,4,3,2,1,0:T(8,128)(2,1)}, bf16[3,2,3...) custom-call(bf16[7,7,64,128]{3,2,1,0:T(8,128)(2,1)S(1)} %get-tuple-e, ...), custom_call_target="tpu_custom_call" | custom-call | tf_op jit(solution)/shard_map/pallas_call | solution.py:1062
  (2 shorter events, 0.0 us)
Async XLA Ops:
  0.7 121.3 %copy-start = (f32[3,3,64,128]{3,2,1,0:T(8,128)S(1)}, f32[3,3,64,128]{3,2,1,0:T(8,128)}, u32[]{:S(2)}) copy-start(f32[3,3,64,128]{3,2,1,0:T(8,128)} %refs_8_.1) | copy-start | bytes 884740
  0.7 121.3 %copy-start.1 = (f32[3,3,64,128]{3,2,1,0:T(8,128)S(1)}, f32[3,3,64,128]{3,2,1,0:T(8,128)}, u32[]{:S(2)}) copy-start(f32[3,3,64,128]{3,2,1,0:T(8,128)} %refs_12_.1) | copy-start | bytes 884740
  0.7 121.3 %copy-start.2 = (f32[3,3,64,128]{3,2,1,0:T(8,128)S(1)}, f32[3,3,64,128]{3,2,1,0:T(8,128)}, u32[]{:S(2)}) copy-start(f32[3,3,64,128]{3,2,1,0:T(8,128)} %refs_16_.1) | copy-start | bytes 884740
  0.7 121.3 %copy-start.3 = (f32[3,3,32,128]{3,2,1,0:T(8,128)S(1)}, f32[3,3,32,128]{3,2,1,0:T(8,128)}, u32[]{:S(2)}) copy-start(f32[3,3,32,128]{3,2,1,0:T(8,128)} %refs_7_.1) | copy-start | bytes 442372
  0.7 121.3 %copy-start.4 = (f32[3,3,32,128]{3,2,1,0:T(8,128)S(1)}, f32[3,3,32,128]{3,2,1,0:T(8,128)}, u32[]{:S(2)}) copy-start(f32[3,3,32,128]{3,2,1,0:T(8,128)} %refs_11_.1) | copy-start | bytes 442372
  0.7 121.3 %copy-start.5 = (f32[3,3,32,128]{3,2,1,0:T(8,128)S(1)}, f32[3,3,32,128]{3,2,1,0:T(8,128)}, u32[]{:S(2)}) copy-start(f32[3,3,32,128]{3,2,1,0:T(8,128)} %refs_15_.1) | copy-start | bytes 442372
  0.7 121.3 %copy-start.6 = (f32[32,128]{1,0:T(8,128)S(1)}, f32[32,128]{1,0:T(8,128)}, u32[]{:S(2)}) copy-start(f32[32,128]{1,0:T(8,128)} %refs_9_.1) | copy-start | bytes 49156
  0.7 121.3 %copy-start.7 = (f32[32,128]{1,0:T(8,128)S(1)}, f32[32,128]{1,0:T(8,128)}, u32[]{:S(2)}) copy-start(f32[32,128]{1,0:T(8,128)} %refs_13_.1) | copy-start | bytes 49156
  0.7 121.3 %copy-start.8 = (f32[32,128]{1,0:T(8,128)S(1)}, f32[32,128]{1,0:T(8,128)}, u32[]{:S(2)}) copy-start(f32[32,128]{1,0:T(8,128)} %refs_17_.1) | copy-start | bytes 49156
  0.8 121.3 %copy-start.9 = (f32[6,128]{1,0:T(8,128)S(1)}, f32[6,128]{1,0:T(8,128)}, u32[]{:S(2)}) copy-start(f32[6,128]{1,0:T(8,128)} %refs_10_.1) | copy-start | bytes 9220
  0.8 121.3 %copy-start.10 = (f32[6,128]{1,0:T(8,128)S(1)}, f32[6,128]{1,0:T(8,128)}, u32[]{:S(2)}) copy-start(f32[6,128]{1,0:T(8,128)} %refs_14_.1) | copy-start | bytes 9220
  0.8 121.3 %copy-start.11 = (f32[6,128]{1,0:T(8,128)S(1)}, f32[6,128]{1,0:T(8,128)}, u32[]{:S(2)}) copy-start(f32[6,128]{1,0:T(8,128)} %refs_18_.1) | copy-start | bytes 9220

commit v4 on v3

--- a/solution.py
+++ b/solution.py
@@ -19,7 +19,7 @@
 MESH = pl.DeviceIdType.MESH
 BF16 = jnp.bfloat16
 F32 = jnp.float32
-COPIES = 192
+COPIES = 240
 VMEM_BYTES = 58 << 20
 
 
@@ -63,6 +63,8 @@
     x_peer = (b + 2 - 4 * x, z)
     y_peer = (b + 4 - 8 * y, z)
     sibling = (b + 1 - 2 * core, z)
+    odd, upper = lax.rem(z, 2), lax.div(z, 2)
+    pair_peer, cross_peer = (b, z + 1 - 2 * odd), (b, lax.rem(z + 2, 4))
     z_peers = [(b, lax.rem(z + d, 4)) for d in (1, 2, 3)]
     b_peers = [(lax.rem(b + d, 8), z) for d in range(1, 8)]
     lanes = lambda which: pl.ds(pl.multiple_of(which * 128, 128), 128)
@@ -191,25 +193,25 @@
             )
 
     big_parts = ((0, 4), (4, ob - 4))
+    out_parts = ((0, 3), (3, 2), (5, ob - 5))
     one_a.near()
     one_b.near()
     one_a.far()
     one_c.near()
     one_b.far()
+    one_c.far()
     two_a.near()
-    one_c.far()
-    two_b.near()
-    slopes_over_z(slo_big, sl_big, *big_parts[0], nb_img)
     one_a.last()
     one_b.last()
     one_c.last()
+    two_b.near()
+    slopes_over_z(slo_big, sl_big, *big_parts[0], nb_img)
     finish(z_norms)
     gains = [
         jnp.concatenate([norms[q, r : r + 1, :] for q in range(4)], axis=1) for r in range(6)
     ]
     for copy in loads[4:]:
         copy.wait()
-    two_c.near()
     one_a.done()
     one_b.done()
     one_c.done()
@@ -289,21 +291,22 @@
         else:
             ref[...] += term
 
-    for ta in range(3):
-        conv_row(first_pre, x_window, w1, 256, ta)
+    conv_row(first_pre, x_window, w1, 256, 0)
+    conv_row(first_pre, x_window, w1, 256, 1)
+    two_a.far()
+    conv_row(first_pre, x_window, w1, 256, 2)
+    first_big, first_small = moments(first_pre)
+    copies = reduce_start(0, first_big + first_small)
     proj_pre[...] = dot(x_window(1, 1), w1[9].reshape(256, 512))
-    first_big, first_small = moments(first_pre)
     side_big, side_small = moments(proj_pre)
-    copies = reduce_start(0, first_big + first_small + side_big + side_small)
-    two_a.far()
+    two_c.near()
     two_b.far()
-    copies = reduce_middle(0, 8, copies)
+    copies = reduce_middle(0, 4, copies)
     slopes_over_z(slo_big, sl_big, *big_parts[1], nb_img)
     slopes_over_z(slo_small, sl_small, 0, os_, ns_img)
     two_a.last()
     two_c.far()
-    two_b.last()
-    sums = reduce_end(0, 8, copies)
+    sums = reduce_end(0, 4, copies)
 
     def centered(total, square, number):
         center = total / number
@@ -311,7 +314,7 @@
 
     numbers = (number_big, number_small)
     first_stat = [centered(sums[2 * g], sums[2 * g + 1], numbers[g]) for g in range(2)]
-    side_stat = [centered(sums[4 + 2 * g], sums[5 + 2 * g], numbers[g]) for g in range(2)]
+    side_copies = reduce_start(4, side_big + side_small)
 
     def place(group, i, value, big, small, shift):
         if group == 0:
@@ -332,22 +335,31 @@
     over_groups(hide, 0)
 
     two_a.done()
+    two_b.last()
     conv_row(second_pre, h_window, w2, 512, 0)
-    two_c.last()
     two_b.done()
     conv_row(second_pre, h_window, w2, 512, 1)
+    side_copies = reduce_middle(4, 4, side_copies)
+    two_c.last()
     two_c.done()
     conv_row(second_pre, h_window, w2, 512, 2)
     second_big, second_small = moments(second_pre)
     copies = reduce_start(1, second_big + second_small)
 
     def prepare(group, i, rows, carry):
-        proj_pre[rows, :] = normed(proj_pre, side_stat[group], rows)
         act[rows, :] = silu_slope(first_pre[rows, :] * gains[0] + gains[1])
         return carry
 
     over_groups(prepare, 0)
     copies = reduce_middle(1, 4, copies)
+    sums = reduce_end(4, 4, side_copies)
+    side_stat = [centered(sums[2 * g], sums[2 * g + 1], numbers[g]) for g in range(2)]
+
+    def prepare_side(group, i, rows, carry):
+        proj_pre[rows, :] = normed(proj_pre, side_stat[group], rows)
+        return carry
+
+    over_groups(prepare_side, 0)
     finish(slope_copies)
     sums = reduce_end(1, 4, copies)
     second_stat = [centered(sums[2 * g], sums[2 * g + 1], numbers[g]) for g in range(2)]
@@ -385,22 +397,29 @@
             target.at[:, :, pl.ds(pl.multiple_of(z * images, images), images)],
         )
     sums_outer = reduce_end(2, 6, copies)
+    outputs_over_z(os_big, out_big, *out_parts[0], nb_img)
 
     def slopes(group, i, rows, carry):
         total, cross_two, cross_side = sums_outer[3 * group : 3 * group + 3]
         number = numbers[group]
         base = work[rows, :] - total / number
         slope_two = gains[2] * second_stat[group][1] * (base - second_pre[rows, :] * (cross_two / number))
+        place(group, i, slope_two.astype(BF16), t_big, t_small, 1)
+        return carry
+
+    def slopes_side(group, i, rows, carry):
+        total, cross_two, cross_side = sums_outer[3 * group : 3 * group + 3]
+        number = numbers[group]
+        base = work[rows, :] - total / number
         slope_side = gains[4] * side_stat[group][1] * (base - proj_pre[rows, :] * (cross_side / number))
-        place(group, i, slope_two.astype(BF16), t_big, t_small, 1)
         place(group, i, slope_side.astype(BF16), p_big, p_small, 0)
         return carry
 
     over_groups(slopes, 0)
 
     class Scatter:
-        def __init__(self, bufs, lo, n):
-            self.bufs, self.taps = bufs, pl.ds(lo, n)
+        def __init__(self, bufs, lo, n, pairs=False):
+            self.bufs, self.taps, self.pairs = bufs, pl.ds(lo, n), pairs
             self.loop = lambda body: lax.fori_loop(lo, lo + n, lambda t, c: (body(t), c)[1], 0)
             a, r = bufs[0], bufs[1]
             self.copies = [send(a.at[self.taps, :, :, 1 - core], r.at[self.taps], sibling)]
@@ -443,14 +462,27 @@
                 c[t, :, 256:512] = (ry[t, x].astype(F32) + rxx[t].astype(F32)).astype(BF16)
 
             self.loop(add)
-            self.copies = [
-                send(
-                    c.at[self.taps, :, lanes(lax.rem(z + d, 4))],
-                    rz.at[d - 1, self.taps],
-                    (b, lax.rem(z + d, 4)),
-                )
-                for d in (1, 2, 3)
-            ]
+            to_z = lambda d: c.at[self.taps, :, lanes(lax.rem(z + d, 4))]
+            if self.pairs:
+                self.copies = [
+                    send(c.at[self.taps, :, lanes(2 * far + 1 - odd)], rz.at[far, self.taps], pair_peer)
+                    for far in range(2)
+                ]
+            else:
+                self.copies = [
+                    send(to_z(d), rz.at[d - 1, self.taps], (b, lax.rem(z + d, 4))) for d in (1, 2, 3)
+                ]
+
+        def cross(self):
+            finish(self.copies)
+            c, rz = self.bufs[6:8]
+
+            def add(t):
+                kept = c[t, :, lanes(2 * (1 - upper) + odd)].astype(F32)
+                rz[1 - upper, t] = (rz[1 - upper, t].astype(F32) + kept).astype(BF16)
+
+            self.loop(add)
+            self.copies = [send(rz.at[1 - upper, self.taps], rz.at[2, self.taps], cross_peer)]
 
         def end(self):
             finish(self.copies)
@@ -458,8 +490,11 @@
 
             def add(t):
                 total = c[t, :, mine].astype(F32)
-                for d in range(3):
-                    total = total + rz[d, t].astype(F32)
+                if self.pairs:
+                    total = total + rz[upper, t].astype(F32) + rz[2, t].astype(F32)
+                else:
+                    for d in range(3):
+                        total = total + rz[d, t].astype(F32)
                 out[t] = total
 
             self.loop(add)
@@ -468,17 +503,21 @@
     s_flat = lambda: both(s_big[0:ob, 0:ob], s_small[0:os_, 0:os_])
     p_flat = lambda: both(p_big[...], p_small[...])
 
-    def grad_two(lo, n):
+    def grad_two(lo, n, pairs=False):
         for t in range(lo, lo + n):
             a2[t] = dot_rows(h_window(t // 3, t % 3), t_flat()).astype(BF16).reshape(a2.shape[1:])
-        return Scatter((a2, r2, rx2, ry2, rxx2, ryy2, c2, rz2, grad_two_out), lo, n)
-
-    def grad_one(ta, proj):
-        sums = dot_rows(row_of(x_window, ta), s_flat()).astype(BF16)
-        a1[3 * ta : 3 * ta + 3] = sums.reshape((3,) + a1.shape[1:])
-        if proj:
-            a1[9] = dot_rows(x_window(1, 1), p_flat()).astype(BF16).reshape(a1.shape[1:])
-        return Scatter((a1, r1, rx1, ry1, rxx1, ryy1, c1, rz1, grad_one_out), 3 * ta, 4 if proj else 3)
+        return Scatter((a2, r2, rx2, ry2, rxx2, ryy2, c2, rz2, grad_two_out), lo, n, pairs)
+
+    one_bufs = (a1, r1, rx1, ry1, rxx1, ryy1, c1, rz1, grad_one_out)
+
+    def grad_one(lo, n):
+        windows = jnp.concatenate([x_window(t // 3, t % 3) for t in range(lo, lo + n)], axis=1)
+        a1[lo : lo + n] = dot_rows(windows, s_flat()).astype(BF16).reshape((n,) + a1.shape[1:])
+        return Scatter(one_bufs, lo, n)
+
+    def grad_proj():
+        a1[9] = dot_rows(x_window(1, 1), p_flat()).astype(BF16).reshape(a1.shape[1:])
+        return Scatter(one_bufs, 9, 1)
 
     def back_row(ta):
         term = None
@@ -486,57 +525,68 @@
             part = dot_t(t_window(ta, tb), w2[3 * ta + tb].reshape(512, 512))
             term = part if term is None else term + part
         if ta == 0:
-            work[...] = term
+            second_pre[...] = term
         else:
-            work[...] += term
-
-    sum_a = grad_two(0, 2)
-    sum_b = grad_two(2, 2)
+            second_pre[...] += term
+
+    sum_a = grad_two(0, 1)
+    sum_b = grad_two(1, 2)
     sum_a.near()
     back_row(0)
     sum_b.near()
-    outputs_over_z(os_big, out_big, *big_parts[0], nb_img)
     back_row(1)
+    sum_a.far()
     back_row(2)
 
     def inner(group, i, rows, carry):
-        e = work[rows, :] * act[rows, :]
-        work[rows, :] = e
+        e = second_pre[rows, :] * act[rows, :]
+        second_pre[rows, :] = e
         return (carry[0] + fold(e), carry[1] + fold(e * first_pre[rows, :]))
 
     inner_big, inner_small = over_groups(inner, 2)
     copies = reduce_start(3, inner_big + inner_small)
-    sum_a.far()
-    sum_c = grad_two(4, 2)
+    sum_c = grad_two(3, 2)
     sum_b.far()
-    sum_d = grad_two(6, 3)
+    sum_d = grad_two(5, 2)
+    copies = reduce_middle(3, 4, copies)
+    outputs_over_z(os_big, out_big, *out_parts[1], nb_img)
     sum_c.near()
-    copies = reduce_middle(3, 4, copies)
+    sum_e = grad_two(7, 2)
     sum_d.near()
+    over_groups(slopes_side, 0)
+    sums_inner = reduce_end(3, 4, copies)
     sum_a.over_z()
     sum_b.over_z()
-    sums_inner = reduce_end(3, 4, copies)
+    outputs_over_z(os_big, out_big, *out_parts[2], nb_img)
 
     def slopes_one(group, i, rows, carry):
         total, cross = sums_inner[2 * group : 2 * group + 2]
         number = numbers[group]
         slope = gains[0] * first_stat[group][1] * (
-            work[rows, :] - total / number - first_pre[rows, :] * (cross / number)
+            second_pre[rows, :] - total / number - first_pre[rows, :] * (cross / number)
         )
         place(group, i, slope.astype(BF16), s_big, s_small, 0)
         return carry
 
     over_groups(slopes_one, 0)
 
-    sum_e = grad_one(0, False)
-    outputs_over_z(os_big, out_big, *big_parts[1], nb_img)
+    sum_f = grad_one(0, 2)
+    sum_e.near()
     sum_c.far()
-    sum_f = grad_one(1, False)
-    sum_e.near()
-    sum_g = grad_one(2, True)
+    sum_g = grad_one(2, 3)
     sum_f.near()
     sum_d.far()
+    sum_p = grad_proj()
+    sum_h = grad_one(5, 3)
     sum_g.near()
+    sum_p.near()
+    sum_c.over_z()
+    sum_e.far()
+    sum_i = grad_one(8, 1)
+    sum_f.far()
+    sum_h.near()
+    sum_i.near()
+    sum_d.over_z()
 
     def back_one(hp, wp):
         total = dot_t(p_flat(), w1[9].reshape(256, 512)) if hp + wp == 0 else None
@@ -551,12 +601,18 @@
         grad_small[:, hp, :, wp] = total[rows_b:].reshape(os_, os_, ns_img, 256)
 
     back_one(0, 0)
+    sum_g.far()
+    sum_p.far()
+    sum_e.over_z()
     back_one(0, 1)
-    sum_e.far()
+    sum_f.over_z()
+    sum_h.far()
+    sum_i.far()
     back_one(1, 0)
-    sum_f.far()
-    sum_c.over_z()
-    sum_g.far()
+    sum_p.over_z()
+    sum_g.over_z()
+    sum_h.over_z()
+    sum_i.over_z()
     back_one(1, 1)
     rows = [
         sums_inner[1] + sums_inner[3],
@@ -569,17 +625,16 @@
     for r, row in enumerate(rows):
         norm_rows[r : r + 1, :] = row
     grad_norms[...] = norm_rows[0:6, mine]
-    sum_d.over_z()
-    sum_e.over_z()
-    sum_f.over_z()
     sum_a.end()
     sum_b.end()
-    sum_g.over_z()
     sum_c.end()
     sum_d.end()
     sum_e.end()
     sum_f.end()
+    sum_p.end()
     sum_g.end()
+    sum_h.end()
+    sum_i.end()
     finish(stores)
     for copy in loads[14:]:
         copy.wait()
@@ -1024,8 +1079,8 @@
         + [
             pltpu.VMEM((4, 8, 128), F32),
             pltpu.VMEM((8, 512), F32),
-            pltpu.VMEM((4, 8, 8, 512), F32),
-            pltpu.VMEM((4, 4, 8, 512), F32),
+            pltpu.VMEM((5, 8, 8, 512), F32),
+            pltpu.VMEM((5, 4, 8, 512), F32),
         ]
         + sum_buffers(10, r1)
         + sum_buffers(9, r2)

time: 125 us -> 119 us (0.952)
  Pallas kernels: 124 us -> 118 us
    pallas_call x1, Pallas kernels: 121 us -> 115 us  [fused_body(): pl.pallas_call(functools.partial(block_kernel, cfg), out_shape=out_shape,...]
where the time goes in v4:
time: 119 us
  Pallas kernels  118 us (99%)
    pallas_call x1, Pallas kernels, fused_body(): pl.pallas_call(functools.partial(block_kernel, cfg), out_shape=out_shape,...  115 us
    pallas_call x1, Pallas kernels, fused_body(): pl.pallas_call(update_kernel, out_shape=[shape(v.shape, v.dtype) for v in...  3.03 us

profile of v4, /device:TPU:0, one launch (start us, length us, event | category | flops | bytes accessed | tf_op | source)
XLA Modules:
  0.0 119.1 jit_solution(5950375298306228260)
XLA Ops:
  0.7 0.0 copy-start
  0.7 0.0 copy-start.1
  0.7 0.0 copy-start.2
  0.7 0.0 copy-start.3
  0.7 0.0 copy-start.4
  0.7 0.0 copy-start.5
  0.7 0.0 copy-start.6
  0.7 0.0 copy-start.7
  0.7 0.0 copy-start.8
  0.8 0.0 copy-start.9
  0.8 0.0 copy-start.10
  0.8 0.0 copy-start.11
  0.8 115.0 %shard_map.311 = (bf16[7,7,64,128]{3,2,1,0:T(8,128)(2,1)S(1)}, bf16[3,3,128,128]{3,2,1,0:T(8,128)(2,1)S(1)}, bf16[7,2,7,2,16,256]{5,4,3,2,1,0:T(8,128)(2,1)S(1)}...) custom-call(bf16[7,2,7,2,16,256]{5,4,3,2,1,0:T(8,128)(2,1)} %bitcast, ...), custom_call_target="tpu_custom_call" | custom-call | flops 23605542912 | bytes 8388608 | tf_op jit(solution)/shard_map/pallas_call | solution.py:1094
  115.8 0.0 copy-done
  115.8 0.0 copy-done.1
  115.8 0.0 copy-done.2
  115.8 0.0 copy-done.3
  115.9 0.0 copy-done.4
  115.9 0.0 copy-done.5
  115.9 0.0 copy-done.6
  115.9 0.0 copy-done.7
  115.9 0.0 copy-done.8
  115.9 0.0 copy-done.9
  115.9 3.0 %shard_map.312 = (bf16[7,7,64,128]{3,2,1,0:T(8,128)(2,1)}, bf16[3,3,128,128]{3,2,1,0:T(8,128)(2,1)}, bf16[7,2,7,2,16,256]{5,4,3,2,1,0:T(8,128)(2,1)}, bf16[3,2,3...) custom-call(bf16[7,7,64,128]{3,2,1,0:T(8,128)(2,1)S(1)} %get-tuple-e, ...), custom_call_target="tpu_custom_call" | custom-call | tf_op jit(solution)/shard_map/pallas_call | solution.py:1117
  (2 shorter events, 0.0 us)
Async XLA Ops:
  0.7 115.2 %copy-start = (f32[3,3,64,128]{3,2,1,0:T(8,128)S(1)}, f32[3,3,64,128]{3,2,1,0:T(8,128)}, u32[]{:S(2)}) copy-start(f32[3,3,64,128]{3,2,1,0:T(8,128)} %refs_8_.1) | copy-start | bytes 884740
  0.7 115.2 %copy-start.1 = (f32[3,3,64,128]{3,2,1,0:T(8,128)S(1)}, f32[3,3,64,128]{3,2,1,0:T(8,128)}, u32[]{:S(2)}) copy-start(f32[3,3,64,128]{3,2,1,0:T(8,128)} %refs_12_.1) | copy-start | bytes 884740
  0.7 115.2 %copy-start.2 = (f32[3,3,64,128]{3,2,1,0:T(8,128)S(1)}, f32[3,3,64,128]{3,2,1,0:T(8,128)}, u32[]{:S(2)}) copy-start(f32[3,3,64,128]{3,2,1,0:T(8,128)} %refs_16_.1) | copy-start | bytes 884740
  0.7 115.2 %copy-start.3 = (f32[3,3,32,128]{3,2,1,0:T(8,128)S(1)}, f32[3,3,32,128]{3,2,1,0:T(8,128)}, u32[]{:S(2)}) copy-start(f32[3,3,32,128]{3,2,1,0:T(8,128)} %refs_7_.1) | copy-start | bytes 442372
  0.7 115.2 %copy-start.4 = (f32[3,3,32,128]{3,2,1,0:T(8,128)S(1)}, f32[3,3,32,128]{3,2,1,0:T(8,128)}, u32[]{:S(2)}) copy-start(f32[3,3,32,128]{3,2,1,0:T(8,128)} %refs_11_.1) | copy-start | bytes 442372
  0.7 115.2 %copy-start.5 = (f32[3,3,32,128]{3,2,1,0:T(8,128)S(1)}, f32[3,3,32,128]{3,2,1,0:T(8,128)}, u32[]{:S(2)}) copy-start(f32[3,3,32,128]{3,2,1,0:T(8,128)} %refs_15_.1) | copy-start | bytes 442372
  0.7 115.2 %copy-start.6 = (f32[32,128]{1,0:T(8,128)S(1)}, f32[32,128]{1,0:T(8,128)}, u32[]{:S(2)}) copy-start(f32[32,128]{1,0:T(8,128)} %refs_9_.1) | copy-start | bytes 49156
  0.7 115.2 %copy-start.7 = (f32[32,128]{1,0:T(8,128)S(1)}, f32[32,128]{1,0:T(8,128)}, u32[]{:S(2)}) copy-start(f32[32,128]{1,0:T(8,128)} %refs_13_.1) | copy-start | bytes 49156
  0.7 115.2 %copy-start.8 = (f32[32,128]{1,0:T(8,128)S(1)}, f32[32,128]{1,0:T(8,128)}, u32[]{:S(2)}) copy-start(f32[32,128]{1,0:T(8,128)} %refs_17_.1) | copy-start | bytes 49156
  0.8 115.2 %copy-start.9 = (f32[6,128]{1,0:T(8,128)S(1)}, f32[6,128]{1,0:T(8,128)}, u32[]{:S(2)}) copy-start(f32[6,128]{1,0:T(8,128)} %refs_10_.1) | copy-start | bytes 9220
  0.8 115.2 %copy-start.10 = (f32[6,128]{1,0:T(8,128)S(1)}, f32[6,128]{1,0:T(8,128)}, u32[]{:S(2)}) copy-start(f32[6,128]{1,0:T(8,128)} %refs_14_.1) | copy-start | bytes 9220
  0.8 115.2 %copy-start.11 = (f32[6,128]{1,0:T(8,128)S(1)}, f32[6,128]{1,0:T(8,128)}, u32[]{:S(2)}) copy-start(f32[6,128]{1,0:T(8,128)} %refs_18_.1) | copy-start | bytes 9220

commit v5 on v4

--- a/solution.py
+++ b/solution.py
@@ -20,7 +20,7 @@
 BF16 = jnp.bfloat16
 F32 = jnp.float32
 COPIES = 240
-VMEM_BYTES = 58 << 20
+VMEM_BYTES = 56 << 20
 
 
 def silu_slope(values):
@@ -45,8 +45,10 @@
 def block_kernel(
     cfg,
     img_big, img_small, slo_big, slo_small, w1_hbm, w2_hbm, wp_hbm, norms_hbm,
+    f1_hbm, f2_hbm, fp_hbm, fn_hbm, s1_hbm, s2_hbm, sp_hbm, sn_hbm,
     out_big, out_small, grad_big, grad_small, grad_one_out, grad_two_out, grad_norms,
-    w1_in, w2_in, wp_in, norms_in, w1, w2, x_big, x_small, h_big, h_small, first_pre, second_pre, proj_pre, work, act,
+    w1_in, w2_in, wp_in, norms_in, f1, f2, fp, fn, s1, s2, sp, sn,
+    w1, w2, x_big, x_small, h_big, h_small, first_pre, second_pre, proj_pre, work, act,
     sl_big, sl_small, os_big, os_small, t_big, t_small, p_big, p_small, s_big, s_small,
     norms, norm_rows, stat_a, stat_b, a1, r1, rx1, ry1, rxx1, ryy1, c1, rz1,
     a2, r2, rx2, ry2, rxx2, ryy2, c2, rz2,
@@ -113,6 +115,11 @@
         slo_small.at[:, :, pl.ds(pl.multiple_of(z * ns_img, ns_img), ns_img)],
         sl_small.at[:, :, :, mine],
     )
+    for source, held in (
+        (f1_hbm, f1), (f2_hbm, f2), (fp_hbm, fp), (fn_hbm, fn),
+        (s1_hbm, s1), (s2_hbm, s2), (sp_hbm, sp), (sn_hbm, sn),
+    ):
+        load(source, held)
     for copy in loads[:4]:
         copy.wait()
     w1[0:9, y, x, core, :, mine] = w1_in[...].astype(BF16)
@@ -150,6 +157,10 @@
             self.rest.append(send(piece, piece, sibling))
             piece = self.w.at[self.taps, 1 - y, x, core]
             self.rest.append(send(piece, piece, sibling))
+
+        def early(self, count):
+            finish(self.rest[:count])
+            self.rest = self.rest[count:]
 
         def last(self):
             finish([self.far_a, self.far_b])
@@ -182,6 +193,41 @@
         ref[side] = zero((side + 1, images, 512))
         ref[:, side] = zero((side + 1, images, 512))
 
+    def both(big, small):
+        return jnp.concatenate([big.reshape(rows_b, -1), small.reshape(rows_s, -1)], axis=0)
+
+    def x_window(ta, tb):
+        hp, wp, sa, sb = (ta + 1) % 2, (tb + 1) % 2, ta // 2, tb // 2
+        return both(
+            x_big[hp, wp, sa : sa + ob, sb : sb + ob],
+            x_small[hp, wp, sa : sa + os_, sb : sb + os_],
+        )
+
+    def h_window(ta, tb, depth=slice(None)):
+        return both(
+            h_big[ta : ta + ob, tb : tb + ob, :, depth],
+            h_small[ta : ta + os_, tb : tb + os_, :, depth],
+        )
+
+    def t_window(ta, tb):
+        ta, tb = 2 - ta, 2 - tb
+        return both(t_big[ta : ta + ob, tb : tb + ob], t_small[ta : ta + os_, tb : tb + os_])
+
+    def s_window(sa, sb):
+        return both(s_big[sa : sa + ob, sb : sb + ob], s_small[sa : sa + os_, sb : sb + os_])
+
+    def row_of(window, ta):
+        return jnp.concatenate([window(ta, tb) for tb in range(3)], axis=1)
+
+    def dot(left, right):
+        return jnp.dot(left, right, preferred_element_type=F32)
+
+    def dot_t(left, right):
+        return lax.dot_general(left, right, (((1,), (1,)), ((), ())), preferred_element_type=F32)
+
+    def dot_rows(left, right):
+        return lax.dot_general(left, right, (((0,), (0,)), ((), ())), preferred_element_type=F32)
+
     slope_copies = []
 
     def slopes_over_z(source, target, lo, n, images):
@@ -252,38 +298,6 @@
 
         return over_groups(body, 2)
 
-    def both(big, small):
-        return jnp.concatenate([big.reshape(rows_b, -1), small.reshape(rows_s, -1)], axis=0)
-
-    def x_window(ta, tb):
-        hp, wp, sa, sb = (ta + 1) % 2, (tb + 1) % 2, ta // 2, tb // 2
-        return both(
-            x_big[hp, wp, sa : sa + ob, sb : sb + ob],
-            x_small[hp, wp, sa : sa + os_, sb : sb + os_],
-        )
-
-    def h_window(ta, tb):
-        return both(h_big[ta : ta + ob, tb : tb + ob], h_small[ta : ta + os_, tb : tb + os_])
-
-    def t_window(ta, tb):
-        ta, tb = 2 - ta, 2 - tb
-        return both(t_big[ta : ta + ob, tb : tb + ob], t_small[ta : ta + os_, tb : tb + os_])
-
-    def s_window(sa, sb):
-        return both(s_big[sa : sa + ob, sb : sb + ob], s_small[sa : sa + os_, sb : sb + os_])
-
-    def row_of(window, ta):
-        return jnp.concatenate([window(ta, tb) for tb in range(3)], axis=1)
-
-    def dot(left, right):
-        return jnp.dot(left, right, preferred_element_type=F32)
-
-    def dot_t(left, right):
-        return lax.dot_general(left, right, (((1,), (1,)), ((), ())), preferred_element_type=F32)
-
-    def dot_rows(left, right):
-        return lax.dot_general(left, right, (((0,), (0,)), ((), ())), preferred_element_type=F32)
-
     def conv_row(ref, window, w, depth, ta):
         term = dot(row_of(window, ta), w[3 * ta : 3 * ta + 3].reshape(3 * depth, 512))
         if ta == 0:
@@ -335,14 +349,24 @@
     over_groups(hide, 0)
 
     two_a.done()
+    conv_row(second_pre, h_window, w2, 512, 0)
     two_b.last()
-    conv_row(second_pre, h_window, w2, 512, 0)
+
+    def conv_last(blocks):
+        pairs = [(tb, yy, xx) for tb in range(3) for yy, xx in blocks]
+        second_pre[...] += dot(
+            jnp.concatenate([h_window(2, tb, lanes(2 * yy + xx)) for tb, yy, xx in pairs], axis=1),
+            jnp.concatenate([w2[6 + tb, yy, xx].reshape(128, 512) for tb, yy, xx in pairs], axis=0),
+        )
+
+    two_c.early(3)
+    conv_last([(y, x), (y, 1 - x), (1 - y, x)])
+    two_c.last()
     two_b.done()
     conv_row(second_pre, h_window, w2, 512, 1)
     side_copies = reduce_middle(4, 4, side_copies)
-    two_c.last()
     two_c.done()
-    conv_row(second_pre, h_window, w2, 512, 2)
+    conv_last([(1 - y, 1 - x)])
     second_big, second_small = moments(second_pre)
     copies = reduce_start(1, second_big + second_small)
 
@@ -636,7 +660,7 @@
     sum_h.end()
     sum_i.end()
     finish(stores)
-    for copy in loads[14:]:
+    for copy in loads[22:]:
         copy.wait()
     for copy in started:
         copy.wait_send()
@@ -991,8 +1015,7 @@
     ]
     for copy in copies:
         copy.start()
-    w1, w2 = states[0], states[1]
-    grads = (g1[0:9].reshape(w1.shape), g2[...].reshape(w2.shape), g1[9], gn[...])
+    grads = (g1[0:9], g2[...], g1[9], gn[...])
     rates = ((9.0 * C_IN) ** (-0.5), (9.0 * C_OUT) ** (-0.5), (1.0 * C_IN) ** (-0.5), NORM_RATE)
     for i in range(4):
         weight, first, second = (states[i + 4 * k][...] for k in range(3))
@@ -1038,7 +1061,7 @@
         pltpu.VMEM((10, r1, 128), F32),
         pltpu.VMEM((9, r2, 128), F32),
         pltpu.VMEM((6, 128), F32),
-    )
+    ) + tuple(pltpu.VMEM(s, F32) for s in ((9, r1, 128), (9, r2, 128), (r1, 128), (6, 128)) * 3)
 
     def sum_buffers(taps, r):
         return [
@@ -1060,10 +1083,6 @@
 
     scratch = (
         [
-            pltpu.VMEM((9, r1, 128), F32),
-            pltpu.VMEM((9, r2, 128), F32),
-            pltpu.VMEM((r1, 128), F32),
-            pltpu.VMEM((6, 128), F32),
             pltpu.VMEM((10, 2, 2, 2, r1, 512), BF16),
             pltpu.VMEM((9, 2, 2, 2, r2, 512), BF16),
             pltpu.VMEM((2, 2, ob + 1, ob + 1, nb_img, C_IN), BF16),
@@ -1087,15 +1106,15 @@
         + [
             pltpu.SemaphoreType.DMA((COPIES,)),
             pltpu.SemaphoreType.DMA((COPIES,)),
-            pltpu.SemaphoreType.DMA((16,)),
+            pltpu.SemaphoreType.DMA((24,)),
         ]
     )
     macs = rows * 512 * (9 * C_IN + 9 * C_OUT + C_IN) * 3
-    out_big, out_small, grad_big, grad_small, grad_one, grad_two, grad_norms = pl.pallas_call(
+    out_big, out_small, grad_big, grad_small, grad_one, grad_two, grad_norms, *states = pl.pallas_call(
         functools.partial(block_kernel, cfg),
         out_shape=out_shape,
-        in_specs=[hbm] * 8,
-        out_specs=[anywhere] * 2 + [vmem] * 5,
+        in_specs=[hbm] * 16,
+        out_specs=[anywhere] * 2 + [vmem] * 17,
         scratch_shapes=scratch,
         compiler_params=pltpu.CompilerParams(
             collective_id=0, has_side_effects=True, vmem_limit_bytes=VMEM_BYTES
@@ -1110,22 +1129,30 @@
         flat(conv2_weight),
         proj_weight,
         norm_params,
-    )
-    weights = (conv1_weight, conv2_weight, proj_weight, norm_params)
+        flat(first_conv1),
+        flat(first_conv2),
+        first_proj,
+        first_norms,
+        flat(second_conv1),
+        flat(second_conv2),
+        second_proj,
+        second_norms,
+    )
     passed = (out_big, out_small, grad_big, grad_small)
     sums = (grad_one, grad_two, grad_norms)
     out_big, out_small, grad_big, grad_small, *updated = pl.pallas_call(
         update_kernel,
-        out_shape=[shape(v.shape, v.dtype) for v in passed] + [shape(w.shape, F32) for w in weights] * 4,
+        out_shape=[shape(v.shape, v.dtype) for v in passed] + [shape(w.shape, F32) for w in states[:4]] * 4,
         in_specs=[vmem] * 19,
         out_specs=[anywhere] * 4 + [vmem] * 16,
         scratch_shapes=[pltpu.SemaphoreType.DMA((4,))],
         compiler_params=pltpu.CompilerParams(vmem_limit_bytes=16 << 20),
     )(
-        *passed, *sums, *weights,
-        first_conv1, first_conv2, first_proj, first_norms,
-        second_conv1, second_conv2, second_proj, second_norms,
-    )
+        *passed, *sums, *states,
+    )
+    updated = [
+        value.reshape((3, 3) + value.shape[1:]) if value.ndim == 3 else value for value in updated
+    ]
 
     def unparity(images, side):
         images = images.reshape(side, side, images.shape[4], C_IN)

time: 119 us -> 118 us (level)
    pallas_call x1, Pallas kernels: 115 us -> 114 us  [fused_body(): pl.pallas_call(functools.partial(block_kernel, cfg), out_shape=out_shape,...]
where the time goes in v5:
time: 118 us; the launch traced here: 117 us
  Pallas kernels  117 us (99%)
    pallas_call x1, Pallas kernels, fused_body(): pl.pallas_call(functools.partial(block_kernel, cfg), out_shape=out_shape,...  114 us
    pallas_call x1, Pallas kernels, fused_body(): pl.pallas_call(update_kernel, out_shape=[shape(v.shape, v.dtype) for v in...  3.03 us

profile of v5, /device:TPU:0, one launch (start us, length us, event | category | flops | bytes accessed | tf_op | source)
XLA Modules:
  0.0 117.4 jit_solution(12071839678554254632)
XLA Ops:
  0.7 113.5 %shard_map.311 = (bf16[7,7,64,128]{3,2,1,0:T(8,128)(2,1)S(1)}, bf16[3,3,128,128]{3,2,1,0:T(8,128)(2,1)S(1)}, bf16[7,2,7,2,16,256]{5,4,3,2,1,0:T(8,128)(2,1)S(1)}...) custom-call(bf16[7,2,7,2,16,256]{5,4,3,2,1,0:T(8,128)(2,1)} %bitcast, ...), custom_call_target="tpu_custom_call" | custom-call | flops 23605542912 | bytes 8388608 | tf_op jit(solution)/shard_map/pallas_call | solution.py:1113
  114.2 3.0 %shard_map.312 = (bf16[7,7,64,128]{3,2,1,0:T(8,128)(2,1)}, bf16[3,3,128,128]{3,2,1,0:T(8,128)(2,1)}, bf16[7,2,7,2,16,256]{5,4,3,2,1,0:T(8,128)(2,1)}, bf16[3,2,3...) custom-call(bf16[7,7,64,128]{3,2,1,0:T(8,128)(2,1)S(1)} %get-tuple-e, ...), custom_call_target="tpu_custom_call" | custom-call | tf_op jit(solution)/shard_map/pallas_call | solution.py:1143

commit v6 on v5

--- a/solution.py
+++ b/solution.py
@@ -649,6 +649,9 @@
     for r, row in enumerate(rows):
         norm_rows[r : r + 1, :] = row
     grad_norms[...] = norm_rows[0:6, mine]
+    early = len(started) - 40
+    for copy in started[:early]:
+        copy.wait_send()
     sum_a.end()
     sum_b.end()
     sum_c.end()
@@ -662,7 +665,7 @@
     finish(stores)
     for copy in loads[22:]:
         copy.wait()
-    for copy in started:
+    for copy in started[early:]:
         copy.wait_send()
     assert used[0] <= COPIES
 
@@ -1006,24 +1009,27 @@
 
 
 def update_kernel(*refs):
-    passed, sums, states, rest = refs[:4], refs[4:7], refs[7:19], refs[19:]
-    passed_out, outs, (sem,) = rest[:4], rest[4:20], rest[20:]
-    g1, g2, gn = sums
-    copies = [
-        pltpu.make_async_copy(src, dst, sem.at[i])
-        for i, (src, dst) in enumerate(zip(passed, passed_out))
-    ]
-    for copy in copies:
+    passed, (g1, g2, gn), states, rest = refs[:4], refs[4:7], refs[7:19], refs[19:]
+    passed_out, outs, made, sem = rest[:4], rest[4:20], rest[20:32], rest[32]
+    gradients = (g1.at[pl.ds(0, 9)], g2, g1.at[9], gn)
+    copies = []
+
+    def store(src, dst):
+        copy = pltpu.make_async_copy(src, dst, sem.at[len(copies)])
         copy.start()
-    grads = (g1[0:9], g2[...], g1[9], gn[...])
+        copies.append(copy)
+
+    for src, dst in zip(passed + gradients, passed_out + outs[:4]):
+        store(src, dst)
     rates = ((9.0 * C_IN) ** (-0.5), (9.0 * C_OUT) ** (-0.5), (1.0 * C_IN) ** (-0.5), NORM_RATE)
     for i in range(4):
         weight, first, second = (states[i + 4 * k][...] for k in range(3))
-        new, moment, square = adamw_step(
-            weight, grads[i], first, second, rates[i], DECAY if i < 3 else 0.0
+        values = adamw_step(
+            weight, gradients[i][...], first, second, rates[i], DECAY if i < 3 else 0.0
         )
-        for k, value in enumerate((grads[i], new, moment, square)):
-            outs[i + 4 * k][...] = value
+        for k, value in enumerate(values):
+            made[i + 4 * k][...] = value
+            store(made[i + 4 * k], outs[4 + i + 4 * k])
     for copy in copies:
         copy.wait()
 
@@ -1144,8 +1150,8 @@
         update_kernel,
         out_shape=[shape(v.shape, v.dtype) for v in passed] + [shape(w.shape, F32) for w in states[:4]] * 4,
         in_specs=[vmem] * 19,
-        out_specs=[anywhere] * 4 + [vmem] * 16,
-        scratch_shapes=[pltpu.SemaphoreType.DMA((4,))],
+        out_specs=[hbm] * 20,
+        scratch_shapes=[pltpu.VMEM(w.shape, F32) for w in states[:4]] * 3 + [pltpu.SemaphoreType.DMA((20,))],
         compiler_params=pltpu.CompilerParams(vmem_limit_bytes=16 << 20),
     )(
         *passed, *sums, *states,

time: 118 us -> 117 us (level)
  no operation moved by 1% of the time
where the time goes in v6:
time: 117 us
  Pallas kernels  116 us (99%)
    pallas_call x1, Pallas kernels, fused_body(): pl.pallas_call(functools.partial(block_kernel, cfg), out_shape=out_shape,...  113 us
    pallas_call x1, Pallas kernels, fused_body(): pl.pallas_call(update_kernel, out_shape=[shape(v.shape, v.dtype) for v in...  2.49 us

profile of v6, /device:TPU:0, one launch (start us, length us, event | category | flops | bytes accessed | tf_op | source)
XLA Modules:
  0.0 116.6 jit_solution(3567184458734263456)
XLA Ops:
  0.7 113.3 %shard_map.311 = (bf16[7,7,64,128]{3,2,1,0:T(8,128)(2,1)S(1)}, bf16[3,3,128,128]{3,2,1,0:T(8,128)(2,1)S(1)}, bf16[7,2,7,2,16,256]{5,4,3,2,1,0:T(8,128)(2,1)S(1)}...) custom-call(bf16[7,2,7,2,16,256]{5,4,3,2,1,0:T(8,128)(2,1)} %bitcast, ...), custom_call_target="tpu_custom_call" | custom-call | flops 23605542912 | bytes 8388608 | tf_op jit(solution)/shard_map/pallas_call | solution.py:1119
  113.9 2.5 %shard_map.312 = (bf16[7,7,64,128]{3,2,1,0:T(8,128)(2,1)}, bf16[3,3,128,128]{3,2,1,0:T(8,128)(2,1)}, bf16[7,2,7,2,16,256]{5,4,3,2,1,0:T(8,128)(2,1)}, bf16[3,2,3...) custom-call(bf16[7,7,64,128]{3,2,1,0:T(8,128)(2,1)S(1)} %get-tuple-e, ...), custom_call_target="tpu_custom_call" | custom-call | tf_op jit(solution)/shard_map/pallas_call | solution.py:1149

commit v7 on v6

--- a/solution.py
+++ b/solution.py
@@ -239,7 +239,7 @@
             )
 
     big_parts = ((0, 4), (4, ob - 4))
-    out_parts = ((0, 3), (3, 2), (5, ob - 5))
+    out_parts = ((0, 4), (4, 1), (5, ob - 5))
     one_a.near()
     one_b.near()
     one_a.far()

time: 117 us -> 116 us (level)
  no operation moved by 1% of the time
where the time goes in v7:
time: 116 us
  Pallas kernels  115 us (99%)
    pallas_call x1, Pallas kernels, fused_body(): pl.pallas_call(functools.partial(block_kernel, cfg), out_shape=out_shape,...  113 us
    pallas_call x1, Pallas kernels, fused_body(): pl.pallas_call(update_kernel, out_shape=[shape(v.shape, v.dtype) for v in...  2.49 us

profile of v7, /device:TPU:0, one launch (start us, length us, event | category | flops | bytes accessed | tf_op | source)
XLA Modules:
  0.0 116.2 jit_solution(2427937851534979728)
XLA Ops:
  0.7 112.8 %shard_map.311 = (bf16[7,7,64,128]{3,2,1,0:T(8,128)(2,1)S(1)}, bf16[3,3,128,128]{3,2,1,0:T(8,128)(2,1)S(1)}, bf16[7,2,7,2,16,256]{5,4,3,2,1,0:T(8,128)(2,1)S(1)}...) custom-call(bf16[7,2,7,2,16,256]{5,4,3,2,1,0:T(8,128)(2,1)} %bitcast, ...), custom_call_target="tpu_custom_call" | custom-call | flops 23605542912 | bytes 8388608 | tf_op jit(solution)/shard_map/pallas_call | solution.py:1119
  113.5 2.5 %shard_map.312 = (bf16[7,7,64,128]{3,2,1,0:T(8,128)(2,1)}, bf16[3,3,128,128]{3,2,1,0:T(8,128)(2,1)}, bf16[7,2,7,2,16,256]{5,4,3,2,1,0:T(8,128)(2,1)}, bf16[3,2,3...) custom-call(bf16[7,7,64,128]{3,2,1,0:T(8,128)(2,1)S(1)} %get-tuple-e, ...), custom_call_target="tpu_custom_call" | custom-call | tf_op jit(solution)/shard_map/pallas_call | solution.py:1149
